TPU v7x, 32 devices: a whole 2x2x4 slice. The times are simulated.
32 devices in a mesh: blk: 4 (over z), fft: 8 (over y, x, core).
Axes of the slice: x: 2, y: 2, z: 4, core: 2. Of those that a mesh axis runs over, the one named last changes fastest.
Arguments:
- tokens: bfloat16 [4096, 1024], P(('blk', 'fft')), may hold values from -6 to 6
- w_in: bfloat16 [1024, 1536], replicated, may hold values from -0.1875 to 0.1875
- conv_taps: float32 [3, 1536], replicated, may hold values from -3 to 3
- causal_taps: bfloat16 [4096, 512], P(('blk', 'fft')), may hold values from -0.15625 to 0.15625
- anticausal_taps: bfloat16 [4096, 512], P(('blk', 'fft')), may hold values from -0.15625 to 0.15625
- skip_gain: float32 [512], replicated, may hold values from 0.1 to 1.9
- w_out: bfloat16 [512, 1024], replicated, may hold values from -0.25 to 0.25
Outputs:
- mixed_out: bfloat16 [4096, 1024], P(('blk', 'fft'))
All inputs are finite; a program needn't handle non-finite values.
Results may differ from a plain program's by a relative error of at most 0.013.
Values may be sent and summed in bfloat16 or wider, within the bound.
A program may use at most 64 MiB of HBM per device.

v0:
```python
import math

import jax
import jax.numpy as jnp
from jax import lax
from jax.sharding import PartitionSpec as P


def with_halo(cells, sides, width):
    for axis, dim in sides:
        count = lax.axis_size(axis)
        ends = count - 1
        head = lax.slice_in_dim(cells, 0, width, axis=dim)
        tail = lax.slice_in_dim(cells, cells.shape[dim] - width, cells.shape[dim], axis=dim)
        cells = jnp.concatenate(
            [
                lax.ppermute(tail, axis, [(i, (i + 1) % count) for i in range(ends)]),
                cells,
                lax.ppermute(head, axis, [((i + 1) % count, i) for i in range(ends)]),
            ],
            axis=dim,
        )
    return cells


def shortened(x):

    def short(part):
        return part.astype(jnp.bfloat16) if part.dtype == jnp.float32 else part

    return jax.tree.map(short, x)


def log_count(count):
    return count.bit_length() - 1


def dft_matrix(count, sign, scale):
    grid = jnp.arange(count, dtype=jnp.int32)
    angle = (
        sign * 2.0 * math.pi * (grid[:, None] * grid[None, :] % count).astype(jnp.float32) / count
    )
    return (jnp.cos(angle) * scale, jnp.sin(angle) * scale)


def local_convolution(signal_cols, causal_cols, anti_cols):
    seq_len = signal_cols.shape[0]
    width = signal_cols.shape[1]
    length = 2 * seq_len
    rows_p = 2 ** (log_count(length) // 2)
    cols_q = length // rows_p
    high = lax.Precision.HIGHEST
    p_real, p_imag = dft_matrix(rows_p, -1.0, 1.0)
    q_real, q_imag = dft_matrix(cols_q, -1.0, 1.0)
    pp_real, pp_imag = dft_matrix(rows_p, 1.0, 1.0 / length)
    qp_real, qp_imag = dft_matrix(cols_q, 1.0, 1.0)
    k_grid = jnp.arange(rows_p, dtype=jnp.int32)
    n_grid = jnp.arange(cols_q, dtype=jnp.int32)
    tw_angle = (
        -2.0 * math.pi * (k_grid[:, None] * n_grid[None, :] % length).astype(jnp.float32) / length
    )
    tw_cos = jnp.cos(tw_angle)
    tw_sin = jnp.sin(tw_angle)

    def forward(grid_rows):
        half = grid_rows.shape[1]
        b_real = jnp.einsum("kp,cpq->ckq", p_real[:, :half], grid_rows, precision=high)
        b_imag = jnp.einsum("kp,cpq->ckq", p_imag[:, :half], grid_rows, precision=high)
        c_real = b_real * tw_cos - b_imag * tw_sin
        c_imag = b_real * tw_sin + b_imag * tw_cos
        x_real = jnp.einsum("ckq,qr->ckr", c_real, q_real, precision=high) - jnp.einsum(
            "ckq,qr->ckr", c_imag, q_imag, precision=high
        )
        x_imag = jnp.einsum("ckq,qr->ckr", c_real, q_imag, precision=high) + jnp.einsum(
            "ckq,qr->ckr", c_imag, q_real, precision=high
        )
        return (x_real, x_imag)

    sig_grid = signal_cols.T.reshape(width, rows_p // 2, cols_q)
    filt_grid = jnp.concatenate([causal_cols, anti_cols], axis=0).T.reshape(width, rows_p, cols_q)
    s_real, s_imag = forward(sig_grid)
    f_real, f_imag = forward(filt_grid)
    y_real = s_real * f_real - s_imag * f_imag
    y_imag = s_real * f_imag + s_imag * f_real
    d_real = jnp.einsum("ckq,qr->ckr", y_real, qp_real, precision=high) - jnp.einsum(
        "ckq,qr->ckr", y_imag, qp_imag, precision=high
    )
    d_imag = jnp.einsum("ckq,qr->ckr", y_real, qp_imag, precision=high) + jnp.einsum(
        "ckq,qr->ckr", y_imag, qp_real, precision=high
    )
    e_real = d_real * tw_cos + d_imag * tw_sin
    e_imag = d_imag * tw_cos - d_real * tw_sin
    half_rows = rows_p // 2
    out_grid = jnp.einsum("nk,ckq->cnq", pp_real[:half_rows], e_real, precision=high) - jnp.einsum(
        "nk,ckq->cnq", pp_imag[:half_rows], e_imag, precision=high
    )
    return out_grid.reshape(width, seq_len).T


def body(tokens, w_in, conv_taps, causal_taps, anticausal_taps, skip_gain, w_out):
    tok_rows = tokens.shape[0]
    channels = w_out.shape[0]
    groups = lax.axis_size("fft")
    blk_index = lax.axis_index("blk")
    fft_index = lax.axis_index("fft")
    device_index = blk_index * groups + fft_index
    position = device_index * tok_rows + jnp.arange(tok_rows, dtype=jnp.int32)
    proj = jnp.dot(tokens, w_in, preferred_element_type=jnp.float32).astype(jnp.bfloat16)
    framed = with_halo(proj, ((("blk", "fft"), 0),), 1).astype(jnp.float32)
    short = conv_taps[0] * framed[:-2] + conv_taps[1] * framed[1:-1] + conv_taps[2] * framed[2:]
    first = short[:, :channels]
    second = short[:, channels : 2 * channels]
    value_part = short[:, 2 * channels :]
    signal = first * value_part
    anticausal = jnp.where(position[:, None] > 0, anticausal_taps.astype(jnp.float32), 0.0)
    causal = causal_taps.astype(jnp.float32)
    moved = (
        lax.all_to_all(
            signal.astype(jnp.bfloat16), "fft", split_axis=1, concat_axis=0, tiled=True
        ).astype(signal.dtype),
        lax.all_to_all(
            causal.astype(jnp.bfloat16), "fft", split_axis=1, concat_axis=0, tiled=True
        ).astype(causal.dtype),
        lax.all_to_all(
            anticausal.astype(jnp.bfloat16), "fft", split_axis=1, concat_axis=0, tiled=True
        ).astype(anticausal.dtype),
    )
    moved = (
        lax.all_to_all(
            moved[0].astype(jnp.bfloat16), "blk", split_axis=1, concat_axis=0, tiled=True
        ).astype(jnp.float32),
        lax.all_to_all(
            moved[1].astype(jnp.bfloat16), "blk", split_axis=1, concat_axis=0, tiled=True
        ).astype(jnp.float32),
        lax.all_to_all(
            moved[2].astype(jnp.bfloat16), "blk", split_axis=1, concat_axis=0, tiled=True
        ).astype(jnp.float32),
    )
    conv_cols = local_convolution(moved[0], moved[1], moved[2])
    returned = lax.all_to_all(
        shortened(conv_cols), "blk", split_axis=0, concat_axis=1, tiled=True
    ).astype(conv_cols.dtype)
    convolved = lax.all_to_all(
        shortened(returned), "fft", split_axis=0, concat_axis=1, tiled=True
    ).astype(returned.dtype)
    convolved = convolved + skip_gain * signal
    gated = (second * convolved).astype(jnp.bfloat16)
    return jnp.dot(gated, w_out, preferred_element_type=jnp.float32).astype(jnp.bfloat16)


def solution(mesh):
    in_specs = (
        P(("blk", "fft"), None),
        P(),
        P(),
        P(("blk", "fft"), None),
        P(("blk", "fft"), None),
        P(),
        P(),
    )
    out_specs = P(("blk", "fft"), None)
    return jax.shard_map(body, mesh=mesh, in_specs=in_specs, out_specs=out_specs, check_vma=False)
```

profile of v0, /device:TPU:0, one launch (start us, length us, event | category | flops | bytes accessed | tf_op | source)
XLA Modules:
  0.0 103.0 jit_solution(17308857740292973029)
XLA Ops:
  0.0 1.8 %copy.43 = bf16[128,512]{0,1:T(8,128)(2,1)} copy(bf16[128,512]{1,0:T(8,128)(2,1)} %param.10) | data formatting | bytes 262144 | tf_op args[3]
  1.8 5.2 %all-to-all-start.2 = ((bf16[128,8,64]{0,2,1:T(8,128)(2,1)}), bf16[128,8,64]{0,2,1:T(8,128)(2,1)}, u32[]{:S(2)}, u32[]{:S(2)}) async-start(bf16[128,8,64]{0,2,1:T(8,128)(2,1)} %bitcast.10), calls=%async_computation.2 | async-start | bytes 262144 | tf_op jit(solution)/shard_map/all_to_all | solution.py:121
  7.0 1.5 %convolution_convert_fusion = bf16[128,1536]{1,0:T(8,128)(2,1)S(1)} fusion(bf16[128,1024]{1,0:T(8,128)(2,1)} %param.7, bf16[1024,1536]{1,0:T(8,128)(2,1)S(1)} %copy-done), kind=kOutput, calls=%fused_computation | convolution fusion | flops 402849792 | bytes 3801088 | tf_op jit(solution)/shard_map/dot_general | solution.py:108
  9.1 2.4 %collective-permute-start = (bf16[1,1536]{1,0:T(2,128)(2,1)}, bf16[1,1536]{1,0:T(2,128)(2,1)S(1)}, u32[]{:S(2)}, u32[]{:S(2)}) collective-permute-start(bf16[1,1536]{1,0:T(2,128)(2,1)} %get-tuple-element.10), channel_id=1, source_target_pairs={{0,1},{1,2},{2,3},{3,4},{4,5},{5,6},{6,7},{7,8},{8,9},{9,10},{10,1... | collective-permute-start | bytes 9224 | tf_op jit(solution)/shard_map/ppermute | solution.py:17
  11.5 1.3 %collective-permute-start.1 = (bf16[1,1536]{1,0:T(2,128)(2,1)}, bf16[1,1536]{1,0:T(2,128)(2,1)S(1)}, u32[]{:S(2)}, u32[]{:S(2)}) collective-permute-start(bf16[1,1536]{1,0:T(2,128)(2,1)} %get-tuple-element.11), channel_id=1, source_target_pairs={{1,0},{2,1},{3,2},{4,3},{5,4},{6,5},{7,6},{8,7},{9,8},{10,9},{11,1... | collective-permute-start | bytes 9224 | tf_op jit(solution)/shard_map/ppermute | solution.py:19
  13.4 1.7 %copy.46 = bf16[128,512]{0,1:T(8,128)(2,1)} copy(bf16[128,512]{1,0:T(8,128)(2,1)} %param.11) | data formatting | bytes 262144 | tf_op args[4]
  15.1 1.6 %select_convert_fusion = bf16[128,512]{0,1:T(8,128)(2,1)} fusion(bf16[128,512]{0,1:T(8,128)(2,1)} %copy.46, pred[128]{0:T(512)(128)(4,1)} %add_compare_fusion), kind=kLoop, calls=%fused_computation.37 | loop fusion | flops 196608 | bytes 262272 | tf_op jit(solution)/shard_map/convert_element_type | solution.py:125
  16.6 0.9 slice_reduce_fusion.2
  17.7 1.1 %fusion.1 = f32[128,1536]{1,0:T(8,128)} fusion(f32[130,1536]{1,0:T(8,128)S(1)} %maximum_convert_fusion, f32[1536]{0:T(1024)S(1)} %get-tuple-element.6, f32[1536]{0:T(1024)S(1)} %get-tuple-element.7, f32[1536]{0:T(1024)S(1)} %get-tuple-element.5), kind=kLoop, calls=%fused_computation.15 | loop fusion | flops 983040 | bytes 3164160 | tf_op jit(solution)/shard_map/add | solution.py:110
  18.8 6.1 %all-to-all-start.4 = ((bf16[128,8,64]{0,2,1:T(8,128)(2,1)}), bf16[128,8,64]{0,2,1:T(8,128)(2,1)S(1)}, u32[]{:S(2)}, u32[]{:S(2)}) async-start(bf16[128,8,64]{0,2,1:T(8,128)(2,1)} %bitcast.13), calls=%async_computation.4 | async-start | bytes 262144 | tf_op jit(solution)/shard_map/all_to_all | solution.py:124
  24.9 1.1 %fusion.21 = bf16[128,512]{1,0:T(8,128)(2,1)S(1)} fusion(f32[128,1536]{1,0:T(8,128)} %fusion.1), kind=kLoop, calls=%fused_computation.52 | loop fusion | flops 131072 | bytes 655360 | tf_op jit(solution)/shard_map/convert_element_type | solution.py:119
  26.7 3.7 %all-to-all-done.4 = bf16[128,8,64]{0,2,1:T(8,128)(2,1)S(1)} async-done(((bf16[128,8,64]{0,2,1:T(8,128)(2,1)}), bf16[128,8,64]{0,2,1:T(8,128)(2,1)S(1)}, u32[]{:S(2)}, u32[]{:S(2)}) %all-to-all-start.4) | async-done | bytes 131104 | tf_op jit(solution)/shard_map/all_to_all | solution.py:124
  30.4 3.4 %all-to-all-start = ((bf16[128,8,64]{0,2,1:T(8,128)(2,1)}), bf16[128,8,64]{0,2,1:T(8,128)(2,1)S(1)}, u32[]{:S(2)}, u32[]{:S(2)}) async-start(bf16[128,8,64]{0,2,1:T(8,128)(2,1)} %bitcast.125), calls=%async_computation | async-start | bytes 262144 | tf_op jit(solution)/shard_map/all_to_all | solution.py:118
  33.8 1.6 %copy.44 = bf16[8,128,64]{1,0,2:T(8,128)(2,1)} copy(bf16[8,128,64]{1,2,0:T(8,128)(2,1)} %bitcast.11) | data formatting | bytes 262144 | tf_op jit(solution)/shard_map/all_to_all | solution.py:121
  35.5 1.6 %all_to_all.102 = bf16[1024,4,16]{0,2,1:T(8,128)(2,1)} reshape(bf16[8,128,64]{1,0,2:T(8,128)(2,1)} %copy.44) | data formatting | bytes 262144 | tf_op jit(solution)/shard_map/all_to_all | solution.py:132
  37.1 2.2 %all-to-all-done = bf16[128,8,64]{0,2,1:T(8,128)(2,1)S(1)} async-done(((bf16[128,8,64]{0,2,1:T(8,128)(2,1)}), bf16[128,8,64]{0,2,1:T(8,128)(2,1)S(1)}, u32[]{:S(2)}, u32[]{:S(2)}) %all-to-all-start) | async-done | bytes 131104 | tf_op jit(solution)/shard_map/all_to_all | solution.py:118
  39.3 6.1 %all-to-all-start.3 = ((bf16[1024,4,16]{0,2,1:T(8,128)(2,1)}), bf16[1024,4,16]{0,2,1:T(8,128)(2,1)}, u32[]{:S(2)}, u32[]{:S(2)}) async-start(bf16[1024,4,16]{0,2,1:T(8,128)(2,1)} %all_to_all.102), calls=%async_computation.3 | async-start | bytes 262144 | tf_op jit(solution)/shard_map/all_to_all | solution.py:132
  46.3 1.6 %all_to_all.107 = bf16[1024,4,16]{0,2,1:T(8,128)(2,1)} reshape(bf16[8,128,64]{1,0,2:T(8,128)(2,1)} %copy.47) | data formatting | bytes 262144 | tf_op jit(solution)/shard_map/all_to_all | solution.py:135
  47.9 3.6 %all-to-all-done.3 = bf16[1024,4,16]{0,2,1:T(8,128)(2,1)} async-done(((bf16[1024,4,16]{0,2,1:T(8,128)(2,1)}), bf16[1024,4,16]{0,2,1:T(8,128)(2,1)}, u32[]{:S(2)}, u32[]{:S(2)}) %all-to-all-start.3) | async-done | bytes 131104 | tf_op jit(solution)/shard_map/all_to_all | solution.py:132
  51.5 3.3 %all-to-all-start.5 = ((bf16[1024,4,16]{0,2,1:T(8,128)(2,1)}), bf16[1024,4,16]{0,2,1:T(8,128)(2,1)S(1)}, u32[]{:S(2)}, u32[]{:S(2)}) async-start(bf16[1024,4,16]{0,2,1:T(8,128)(2,1)} %all_to_all.107), calls=%async_computation.5 | async-start | bytes 262144 | tf_op jit(solution)/shard_map/all_to_all | solution.py:135
  56.5 1.6 %all_to_all.95 = bf16[1024,4,16]{0,2,1:T(8,128)(2,1)} reshape(bf16[8,128,64]{1,0,2:T(8,128)(2,1)} %copy.41) | data formatting | bytes 262144 | tf_op jit(solution)/shard_map/all_to_all | solution.py:129
  58.1 1.6 %copy.66 = bf16[4,2,8,1024]{3,2,0,1:T(8,128)(2,1)} copy(bf16[4,2,8,1024]{3,2,1,0:T(8,128)(2,1)} %bitcast.35) | data formatting | bytes 262144 | tf_op jit(solution)/shard_map/convert_element_type | solution.py:134
  59.7 1.0 %all-to-all-done.5 = bf16[1024,4,16]{0,2,1:T(8,128)(2,1)S(1)} async-done(((bf16[1024,4,16]{0,2,1:T(8,128)(2,1)}), bf16[1024,4,16]{0,2,1:T(8,128)(2,1)S(1)}, u32[]{:S(2)}, u32[]{:S(2)}) %all-to-all-start.5) | async-done | bytes 131104 | tf_op jit(solution)/shard_map/all_to_all | solution.py:135
  60.7 4.0 %all-to-all-start.1 = ((bf16[1024,4,16]{0,2,1:T(8,128)(2,1)}), bf16[1024,4,16]{0,2,1:T(8,128)(2,1)S(1)}, u32[]{:S(2)}, u32[]{:S(2)}) async-start(bf16[1024,4,16]{0,2,1:T(8,128)(2,1)} %all_to_all.95), calls=%async_computation.1 | async-start | bytes 262144 | tf_op jit(solution)/shard_map/all_to_all | solution.py:129
  64.8 0.9 maximum_bitcast_fusion
  68.5 1.6 %convolution_add_fusion.1 = f32[16,64,128]{2,1,0:T(8,128)} fusion(f32[16,64,128]{2,1,0:T(8,128)S(1)} %fusion.17, f32[16,64,128]{2,1,0:T(8,128)S(1)} %convolution_bitcast_fusion, f32[16,64,128]{2,1,0:T(8,128)S(1)} %convolution_bitcast_fusion.1, f32[64,128]{1,0:T(8,128)S(1)} %get-tuple-element.12, f32[64,128]{1,0:T(8,128)S(1)} %get-tuple-element.13), kind=kOutput, calls=%fused_computation.7 | convolution fusion | flops 202080256 | bytes 2162688 | tf_op jit(solution)/shard_map/ckq,qr->ckr/dot_general | solution.py:74
  70.2 1.6 %convolution_subtract_fusion.1 = f32[16,64,128]{2,1,0:T(8,128)} fusion(f32[16,64,128]{2,1,0:T(8,128)S(1)} %fusion.18, f32[16,64,128]{2,1,0:T(8,128)S(1)} %convolution_bitcast_fusion, f32[16,64,128]{2,1,0:T(8,128)S(1)} %convolution_bitcast_fusion.1, f32[64,128]{1,0:T(8,128)S(1)} %get-tuple-element.12, f32[64,128]{1,0:T(8,128)S(1)} %get-tuple-element.13), kind=kOutput, calls=%fused_computation.9 | convolution fusion | flops 202080256 | bytes 2162688 | tf_op jit(solution)/shard_map/ckq,qr->ckr/dot_general | solution.py:71
  75.2 0.9 multiply_add_fusion
  80.7 10.8 %all_to_all.122 = bf16[4,1024,16]{1,2,0:T(8,128)(2,1)S(1)} all-to-all(bf16[4,1024,16]{1,2,0:T(8,128)(2,1)S(1)} %bitcast.128), channel_id=1, replica_groups=mesh['blk'=4,'fft'=8] {'blk'}, dimensions={0} | all-to-all | bytes 262144 | tf_op jit(solution)/shard_map/all_to_all | solution.py:140
  91.6 7.9 %all_to_all.123 = bf16[8,128,64]{1,2,0:T(8,128)(2,1)S(1)} all-to-all(bf16[8,128,64]{1,2,0:T(8,128)(2,1)S(1)} %copy.54), channel_id=1, replica_groups=mesh['blk'=4,'fft'=8] {'fft'}, dimensions={0} | all-to-all | bytes 262144 | tf_op jit(solution)/shard_map/all_to_all | solution.py:143
  99.5 0.9 copy.55
  100.4 2.6 %convolution_convert_fusion.1 = bf16[128,1024]{1,0:T(8,128)(2,1)} fusion(bf16[512,1024]{1,0:T(8,128)(2,1)} %param.13, f32[128,1536]{1,0:T(8,128)} %fusion.1, f32[128,512]{1,0:T(8,128)} %copy.55, f32[512]{0:T(512)S(1)} %copy-done.4), kind=kOutput, calls=%fused_computation.11 | convolution fusion | flops 134676480 | bytes 2361344 | tf_op jit(solution)/shard_map/dot_general | solution.py:148
  (48 shorter events, 15.3 us)
Async XLA Ops:
  0.0 7.0 %copy-start = (bf16[1024,1536]{1,0:T(8,128)(2,1)S(1)}, bf16[1024,1536]{1,0:T(8,128)(2,1)}, u32[]{:S(2)}) copy-start(bf16[1024,1536]{1,0:T(8,128)(2,1)} %param.8) | copy-start | bytes 9437188
  1.8 17.0 %all-to-all-start.2 = ((bf16[128,8,64]{0,2,1:T(8,128)(2,1)}), bf16[128,8,64]{0,2,1:T(8,128)(2,1)}, u32[]{:S(2)}, u32[]{:S(2)}) async-start(bf16[128,8,64]{0,2,1:T(8,128)(2,1)} %bitcast.10), calls=%async_computation.2 | async-start | bytes 262144 | tf_op jit(solution)/shard_map/all_to_all | solution.py:121
  9.1 8.4 %collective-permute-start = (bf16[1,1536]{1,0:T(2,128)(2,1)}, bf16[1,1536]{1,0:T(2,128)(2,1)S(1)}, u32[]{:S(2)}, u32[]{:S(2)}) collective-permute-start(bf16[1,1536]{1,0:T(2,128)(2,1)} %get-tuple-element.10), channel_id=1, source_target_pairs={{0,1},{1,2},{2,3},{3,4},{4,5},{5,6},{6,7},{7,8},{8,9},{9,10},{10,1... | collective-permute-start | bytes 9224 | tf_op jit(solution)/shard_map/ppermute | solution.py:17
  11.5 6.0 %collective-permute-start.1 = (bf16[1,1536]{1,0:T(2,128)(2,1)}, bf16[1,1536]{1,0:T(2,128)(2,1)S(1)}, u32[]{:S(2)}, u32[]{:S(2)}) collective-permute-start(bf16[1,1536]{1,0:T(2,128)(2,1)} %get-tuple-element.11), channel_id=1, source_target_pairs={{1,0},{2,1},{3,2},{4,3},{5,4},{6,5},{7,6},{8,7},{9,8},{10,9},{11,1... | collective-permute-start | bytes 9224 | tf_op jit(solution)/shard_map/ppermute | solution.py:19
  18.8 11.6 %all-to-all-start.4 = ((bf16[128,8,64]{0,2,1:T(8,128)(2,1)}), bf16[128,8,64]{0,2,1:T(8,128)(2,1)S(1)}, u32[]{:S(2)}, u32[]{:S(2)}) async-start(bf16[128,8,64]{0,2,1:T(8,128)(2,1)} %bitcast.13), calls=%async_computation.4 | async-start | bytes 262144 | tf_op jit(solution)/shard_map/all_to_all | solution.py:124
  30.4 8.8 %all-to-all-start = ((bf16[128,8,64]{0,2,1:T(8,128)(2,1)}), bf16[128,8,64]{0,2,1:T(8,128)(2,1)S(1)}, u32[]{:S(2)}, u32[]{:S(2)}) async-start(bf16[128,8,64]{0,2,1:T(8,128)(2,1)} %bitcast.125), calls=%async_computation | async-start | bytes 262144 | tf_op jit(solution)/shard_map/all_to_all | solution.py:118
  39.3 12.2 %all-to-all-start.3 = ((bf16[1024,4,16]{0,2,1:T(8,128)(2,1)}), bf16[1024,4,16]{0,2,1:T(8,128)(2,1)}, u32[]{:S(2)}, u32[]{:S(2)}) async-start(bf16[1024,4,16]{0,2,1:T(8,128)(2,1)} %all_to_all.102), calls=%async_computation.3 | async-start | bytes 262144 | tf_op jit(solution)/shard_map/all_to_all | solution.py:132
  51.5 9.2 %all-to-all-start.5 = ((bf16[1024,4,16]{0,2,1:T(8,128)(2,1)}), bf16[1024,4,16]{0,2,1:T(8,128)(2,1)S(1)}, u32[]{:S(2)}, u32[]{:S(2)}) async-start(bf16[1024,4,16]{0,2,1:T(8,128)(2,1)} %all_to_all.107), calls=%async_computation.5 | async-start | bytes 262144 | tf_op jit(solution)/shard_map/all_to_all | solution.py:135
  60.7 11.1 %all-to-all-start.1 = ((bf16[1024,4,16]{0,2,1:T(8,128)(2,1)}), bf16[1024,4,16]{0,2,1:T(8,128)(2,1)S(1)}, u32[]{:S(2)}, u32[]{:S(2)}) async-start(bf16[1024,4,16]{0,2,1:T(8,128)(2,1)} %all_to_all.95), calls=%async_computation.1 | async-start | bytes 262144 | tf_op jit(solution)/shard_map/all_to_all | solution.py:129
  67.7 4.2 %copy-start.3 = (f32[64,64]{0,1:T(8,128)S(1)}, f32[64,64]{0,1:T(8,128)}, u32[]{:S(2)}) copy-start(f32[64,64]{0,1:T(8,128)} %multiply_sine_fusion.8) | copy-start | bytes 49156
  72.3 2.9 %copy-start.1 = (f32[16,64,128]{2,1,0:T(8,128)S(1)}, f32[16,64,128]{2,1,0:T(8,128)}, u32[]{:S(2)}) copy-start(f32[16,64,128]{2,1,0:T(8,128)} %convolution_add_fusion.1) | copy-start | bytes 1572868
  72.3 2.9 %copy-start.2 = (f32[16,64,128]{2,1,0:T(8,128)S(1)}, f32[16,64,128]{2,1,0:T(8,128)}, u32[]{:S(2)}) copy-start(f32[16,64,128]{2,1,0:T(8,128)} %convolution_subtract_fusion.1) | copy-start | bytes 1572868
  78.6 21.8 %copy-start.4 = (f32[512]{0:T(512)S(1)}, f32[512]{0:T(512)}, u32[]{:S(2)}) copy-start(f32[512]{0:T(512)} %param.12) | copy-start | bytes 6148
where the time goes:
time: 104 us; the launch traced here: 103 us
  starting transfers between devices  31.7 us (30%)
  matrix products  18.8 us (18%)
  blocking collectives  18.7 us (18%)
  local copies, waits for them, and re-layouts  16.4 us (16%)
  waiting for transfers between devices  10.6 us (10%)
  other arithmetic  6.47 us (6%)
    all_to_all x1, blocking collectives, body(): lax.all_to_all(shortened(conv_cols), 'blk', split_axis=0, concat_axis=1,...  10.8 us
    all_to_all x1, blocking collectives, body(): lax.all_to_all(shortened(returned), 'fft', split_axis=0, concat_axis=1, t...  7.92 us
    all_to_all x1, starting transfers between devices, body(): lax.all_to_all(moved[1].astype(jnp.bfloat16), 'blk', split_axis=1, concat...  6.07 us
    all_to_all x1, starting transfers between devices, body(): lax.all_to_all(anticausal.astype(jnp.bfloat16), 'fft', split_axis=1, conc...  6.06 us
    all_to_all x1, starting transfers between devices, body(): lax.all_to_all(causal.astype(jnp.bfloat16), 'fft', split_axis=1, concat_a...  5.17 us
    all_to_all x1, starting transfers between devices, body(): lax.all_to_all(moved[0].astype(jnp.bfloat16), 'blk', split_axis=1, concat...  4.03 us
    all_to_all x1, waiting for transfers between devices, body(): lax.all_to_all(anticausal.astype(jnp.bfloat16), 'fft', split_axis=1, conc...  3.7 us
    all_to_all x1, waiting for transfers between devices, body(): lax.all_to_all(moved[1].astype(jnp.bfloat16), 'blk', split_axis=1, concat...  3.64 us
  transfers between devices with their start and end apart: 8, of which 4 were waited for; matrix products, arithmetic and copies ran while one was open for 22% of the time, Pallas kernels for 0%

commit v1 on v0

--- a/solution.py
+++ b/solution.py
@@ -1,9 +1,16 @@
+import functools
 import math
 
 import jax
 import jax.numpy as jnp
+import ml_dtypes
+import numpy as np
 from jax import lax
+from jax.experimental import pallas as pl
+from jax.experimental.pallas import tpu as pltpu
 from jax.sharding import PartitionSpec as P
+
+MESH = pl.DeviceIdType.MESH
 
 
 def with_halo(cells, sides, width):
@@ -148,6 +155,336 @@
     return jnp.dot(gated, w_out, preferred_element_type=jnp.float32).astype(jnp.bfloat16)
 
 
+def grid_constants(blocks, width):
+    length = 2 * blocks * width
+    half_freq = np.arange(blocks) + 0.5
+
+    def split(mat):
+        high = mat.astype(ml_dtypes.bfloat16)
+        low = (mat - high.astype(np.float64)).astype(ml_dtypes.bfloat16)
+        return high, low
+
+    rows = np.outer(half_freq, np.arange(2 * blocks)) * (2.0 * np.pi / (2 * blocks))
+    flip = np.where(np.arange(2 * blocks) < blocks, 1.0, -1.0)
+    across = np.concatenate([np.cos(rows), -np.sin(rows)], axis=0) * flip
+    across = np.concatenate(split(across), axis=0)
+    turn = np.outer(half_freq, np.arange(width)) * (2.0 * np.pi / length)
+    twist = np.stack([np.cos(turn), np.sin(turn)]).astype(np.float32)
+    grid = np.outer(np.arange(width), np.arange(width)) % width * (2.0 * np.pi / width)
+    cos, sin = np.cos(grid), np.sin(grid)
+    within = np.stack(split(np.block([[cos, -sin], [sin, cos]])))
+    within_back = np.stack(split(np.block([[cos, sin], [-sin, cos]])))
+    back = rows[:, :blocks].T
+    back = np.concatenate([np.cos(back), -np.sin(back)], axis=1) * (2.0 / length)
+    back = np.concatenate(split(back), axis=0)
+    return across, twist, within, within_back, back
+
+
+def dot32(a, b):
+    return jnp.dot(a, b, preferred_element_type=jnp.float32)
+
+
+def halves(x):
+    high = x.astype(jnp.bfloat16)
+    low = (x - high.astype(jnp.float32)).astype(jnp.bfloat16)
+    return high, low
+
+
+def mixer_kernel(
+    blocks,
+    groups,
+    tokens,
+    causal,
+    anti,
+    conv_taps,
+    skip_gain,
+    across,
+    twist,
+    back,
+    w_in_hbm,
+    w_out_hbm,
+    within_hbm,
+    within_back_hbm,
+    out,
+    w_in,
+    w_out,
+    within,
+    within_back,
+    framed,
+    edge_out,
+    edge_in,
+    filt_out,
+    filt_in,
+    sig_out,
+    sig_in,
+    ret_out,
+    ret_in,
+    spread,
+    spectrum,
+    load_sem,
+    edge_send,
+    edge_recv,
+    filt_send,
+    filt_recv,
+    sig_send,
+    sig_recv,
+    ret_send,
+    ret_recv,
+):
+    f32, bf16 = jnp.float32, jnp.bfloat16
+    width, depth = tokens.shape
+    channels = w_out.shape[0]
+    mine = channels // blocks
+    me = lax.axis_index("blk") * groups + lax.axis_index("fft")
+
+    def place(peer):
+        return (peer // groups, peer % groups)
+
+    loads = [
+        pltpu.make_async_copy(src, dst, load_sem.at[i])
+        for i, (src, dst) in enumerate(
+            (
+                (w_in_hbm, w_in),
+                (within_hbm, within),
+                (within_back_hbm, within_back),
+                (w_out_hbm, w_out),
+            )
+        )
+    ]
+    for load in loads:
+        load.start()
+
+    barrier = pltpu.get_barrier_semaphore()
+
+    @pl.loop(1, blocks)
+    def _(i):
+        pl.semaphore_signal(
+            barrier, inc=1, device_id=place((me + i) % blocks), device_id_type=MESH
+        )
+
+    def send_all(src, dst, send_sem, recv_sem):
+        @pl.loop(1, blocks)
+        def _(i):
+            peer = (me + i) % blocks
+            pltpu.make_async_remote_copy(
+                src_ref=src.at[peer],
+                dst_ref=dst.at[me],
+                send_sem=send_sem,
+                recv_sem=recv_sem,
+                device_id=place(peer),
+                device_id_type=MESH,
+            ).start()
+
+        pltpu.make_async_copy(src.at[me], dst.at[me], recv_sem).start()
+
+    def arrived(dst, recv_sem):
+        pltpu.make_async_copy(dst, dst, recv_sem).wait()
+
+    def sent(src, send_sem):
+        most = src.at[pl.ds(0, blocks - 1)]
+        pltpu.make_async_copy(most, most, send_sem).wait()
+
+    edge_out[0] = tokens[width - 16 :, :].astype(f32)[15:16]
+    edge_out[1] = tokens[0:16, :].astype(f32)[0:1]
+    filt_out[:, 0:mine, :] = (
+        causal[...].astype(f32).T.astype(bf16).reshape(blocks, mine, width)
+    )
+    unused = (lax.broadcasted_iota(jnp.int32, anti.shape, 0) == 0) & (me == 0)
+    filt_out[:, mine:, :] = (
+        jnp.where(unused, 0.0, anti[...].astype(f32))
+        .T.astype(bf16)
+        .reshape(blocks, mine, width)
+    )
+    pl.semaphore_wait(barrier, blocks - 1)
+    edges = [
+        pltpu.make_async_remote_copy(
+            src_ref=edge_out.at[i],
+            dst_ref=edge_in.at[i],
+            send_sem=edge_send.at[i],
+            recv_sem=edge_recv.at[i],
+            device_id=place((me + step) % blocks),
+            device_id_type=MESH,
+        )
+        for i, step in ((0, 1), (1, blocks - 1))
+    ]
+    for edge in edges:
+        edge.start()
+    send_all(filt_out, filt_in, filt_send, filt_recv)
+
+    framed[0:width, :] = tokens[...]
+    loads[0].wait()
+    for edge in edges:
+        edge.wait()
+    row16 = lax.broadcasted_iota(jnp.int32, (16, depth), 0)
+    prev = jnp.where(me == 0, 0.0, edge_in[0])
+    following = jnp.where(me == blocks - 1, 0.0, edge_in[1])
+    framed[width:, :] = jnp.where(
+        row16 == 0, prev, jnp.where(row16 == 1, following, 0.0)
+    ).astype(bf16)
+
+    row = lax.broadcasted_iota(jnp.int32, (width, channels), 0)
+
+    def stream(part):
+        cols = slice(part * channels, (part + 1) * channels)
+        proj = dot32(framed[...], w_in[:, cols]).astype(bf16).astype(f32)
+        here = proj[:width]
+        before = jnp.where(row == 0, proj[width : width + 1], pltpu.roll(here, 1, 0))
+        after = jnp.where(
+            row == width - 1, proj[width + 1 : width + 2], pltpu.roll(here, width - 1, 0)
+        )
+        taps = conv_taps[:, cols]
+        return taps[0:1] * before + taps[1:2] * here + taps[2:3] * after
+
+    signal = stream(0) * stream(2)
+    sig_out[...] = signal.T.astype(bf16).reshape(blocks, mine, width)
+    send_all(sig_out, sig_in, sig_send, sig_recv)
+    second = stream(1)
+
+    cos, sin = twist[0], twist[1]
+
+    def lane(x, c):
+        return x[:, c * width : (c + 1) * width]
+
+    def times(x, mats):
+        high, low = halves(x)
+        return dot32(high, mats[0]) + dot32(low, mats[0]) + dot32(high, mats[1])
+
+    def forward(grid, mats):
+        both = dot32(mats, grid)
+        freq = both[: 2 * blocks] + both[2 * blocks :]
+        parts = []
+        for c in range(mine):
+            real, imag = lane(freq[:blocks], c), lane(freq[blocks:], c)
+            parts.append(
+                jnp.concatenate([real * cos + imag * sin, imag * cos - real * sin], axis=1)
+            )
+        return times(jnp.concatenate(parts, axis=0), within)
+
+    loads[1].wait()
+    loads[2].wait()
+    arrived(filt_in, filt_recv)
+    spread[...] = filt_in[...].astype(f32).reshape(2 * blocks * mine, width)
+    grid = jnp.concatenate(
+        [
+            jnp.concatenate(
+                [
+                    spread[pl.ds(c, blocks, stride=2 * mine), :],
+                    spread[pl.ds(mine + c, blocks, stride=2 * mine), :],
+                ],
+                axis=0,
+            ).astype(bf16)
+            for c in range(mine)
+        ],
+        axis=1,
+    )
+    spectrum[...] = forward(grid, across[...])
+
+    arrived(sig_in, sig_recv)
+    spread[0 : blocks * mine, :] = sig_in[...].astype(f32).reshape(blocks * mine, width)
+    grid = jnp.concatenate(
+        [spread[pl.ds(c, blocks, stride=mine), :].astype(bf16) for c in range(mine)], axis=1
+    )
+    sig = forward(grid, across[:, 0:blocks])
+    s_real, s_imag = sig[:, :width], sig[:, width:]
+    f_real, f_imag = spectrum[:, :width], spectrum[:, width:]
+    product = jnp.concatenate(
+        [s_real * f_real - s_imag * f_imag, s_real * f_imag + s_imag * f_real], axis=1
+    )
+    turned = times(product, within_back)
+    parts = []
+    for c in range(mine):
+        rows = turned[c * blocks : (c + 1) * blocks]
+        real, imag = rows[:, :width], rows[:, width:]
+        parts.append(
+            jnp.concatenate([real * cos - imag * sin, imag * cos + real * sin], axis=0)
+        )
+    high, low = halves(jnp.concatenate(parts, axis=1))
+    both = dot32(back[...], high)
+    conv = both[:blocks] + both[blocks:] + dot32(back[0:blocks, :], low)
+    for c in range(mine):
+        spread[pl.ds(c, blocks, stride=mine), :] = lane(conv, c)
+    ret_out[...] = spread[0 : blocks * mine, :].astype(bf16).reshape(blocks, mine, width)
+    send_all(ret_out, ret_in, ret_send, ret_recv)
+
+    direct = skip_gain[...] * signal
+    loads[3].wait()
+    arrived(ret_in, ret_recv)
+    convolved = ret_in[...].astype(f32).reshape(channels, width).T + direct
+    gated = (second * convolved).astype(bf16)
+    out[...] = dot32(gated, w_out[...]).astype(bf16)
+    sent(filt_out, filt_send)
+    sent(sig_out, sig_send)
+    sent(ret_out, ret_send)
+
+
+def one_kernel(tokens, w_in, conv_taps, causal_taps, anticausal_taps, skip_gain, w_out):
+    width, depth = tokens.shape
+    channels = w_out.shape[0]
+    groups = lax.axis_size("fft")
+    blocks = lax.axis_size("blk") * groups
+    mine = channels // blocks
+    across, twist, within, within_back, back = grid_constants(blocks, width)
+    f32, bf16 = jnp.float32, jnp.bfloat16
+    vmem = pl.BlockSpec(memory_space=pltpu.VMEM)
+    whole = pl.BlockSpec(memory_space=pl.ANY)
+    one = pltpu.SemaphoreType.DMA
+    return pl.pallas_call(
+        functools.partial(mixer_kernel, blocks, groups),
+        out_shape=jax.ShapeDtypeStruct((width, w_out.shape[1]), bf16),
+        in_specs=[vmem] * 8 + [whole] * 4,
+        out_specs=vmem,
+        scratch_shapes=[
+            pltpu.VMEM(w_in.shape, bf16),
+            pltpu.VMEM(w_out.shape, bf16),
+            pltpu.VMEM(within.shape, bf16),
+            pltpu.VMEM(within_back.shape, bf16),
+            pltpu.VMEM((width + 16, depth), bf16),
+            pltpu.VMEM((2, 1, depth), f32),
+            pltpu.VMEM((2, 1, depth), f32),
+            pltpu.VMEM((blocks, 2 * mine, width), bf16),
+            pltpu.VMEM((blocks, 2 * mine, width), bf16),
+            pltpu.VMEM((blocks, mine, width), bf16),
+            pltpu.VMEM((blocks, mine, width), bf16),
+            pltpu.VMEM((blocks, mine, width), bf16),
+            pltpu.VMEM((blocks, mine, width), bf16),
+            pltpu.VMEM((2 * blocks * mine, width), f32),
+            pltpu.VMEM((blocks * mine, 2 * width), f32),
+            one((4,)),
+            one((2,)),
+            one((2,)),
+            one,
+            one,
+            one,
+            one,
+            one,
+            one,
+        ],
+        compiler_params=pltpu.CompilerParams(
+            collective_id=0, has_side_effects=True, vmem_limit_bytes=48 * 2**20
+        ),
+    )(
+        tokens,
+        causal_taps,
+        anticausal_taps,
+        conv_taps,
+        skip_gain[None, :],
+        jnp.asarray(across),
+        jnp.asarray(twist),
+        jnp.asarray(back),
+        w_in,
+        w_out,
+        jnp.asarray(within),
+        jnp.asarray(within_back),
+    )
+
+
+def mixer(tokens, w_in, conv_taps, causal_taps, anticausal_taps, skip_gain, w_out):
+    devices = lax.axis_size("blk") * lax.axis_size("fft")
+    fits = tokens.shape[0] == 128 and w_out.shape[0] == 16 * devices
+    chosen = one_kernel if fits else body
+    return chosen(tokens, w_in, conv_taps, causal_taps, anticausal_taps, skip_gain, w_out)
+
+
 def solution(mesh):
     in_specs = (
         P(("blk", "fft"), None),
@@ -159,4 +496,4 @@
         P(),
     )
     out_specs = P(("blk", "fft"), None)
-    return jax.shard_map(body, mesh=mesh, in_specs=in_specs, out_specs=out_specs, check_vma=False)
+    return jax.shard_map(mixer, mesh=mesh, in_specs=in_specs, out_specs=out_specs, check_vma=False)

time: 104 us -> 38.1 us (0.37)
  starting transfers between devices: 31.7 us -> 0 us
  Pallas kernels: 0 us -> 25.3 us
  matrix products: 18.8 us -> 0 us
  blocking collectives: 18.7 us -> 0 us
  waiting for transfers between devices: 10.6 us -> 0 us
  other arithmetic: 6.47 us -> 0 us
  local copies, waits for them, and re-layouts: 16.4 us -> 12.1 us
    all_to_all x6 -> x0, starting transfers between devices: 28 us -> none  [the longest x1 6.07 us: body(): lax.all_to_all(moved[1].astype(jnp.bfloat16), 'blk', split_axis=1, concat...]
    pallas_call x0 -> x1, Pallas kernels: none -> 25.3 us  [one_kernel(): pl.pallas_call(functools.partial(mixer_kernel, blocks, groups), out_shape...]
    dot_general x20 -> x0, matrix products: 18.8 us -> none  [the longest x1 2.6 us: body(): jnp.dot(gated, w_out, preferred_element_type=jnp.float32)]
    all_to_all x2 -> x0, blocking collectives: 18.7 us -> none  [the longest x1 10.8 us: body(): lax.all_to_all(shortened(conv_cols), 'blk', split_axis=0, concat_axis=1,...]
    all_to_all x6 -> x0, waiting for transfers between devices: 10.6 us -> none  [the longest x1 3.7 us: body(): lax.all_to_all(anticausal.astype(jnp.bfloat16), 'fft', split_axis=1, conc...]
    unnamed x16 -> x25, local copies, waits for them, and re-layouts: 3.64 us -> 12.1 us
    all_to_all x9 -> x0, local copies, waits for them, and re-layouts: 8.04 us -> none  [the longest x1 1.65 us: body(): lax.all_to_all(causal.astype(jnp.bfloat16), 'fft', split_axis=1, concat_a...]
    ppermute x2 -> x0, starting transfers between devices: 3.68 us -> none  [the longest x1 2.39 us: with_halo(): lax.ppermute(tail, axis, [(i, (i + 1) % count) for i in range(ends)])]
  transfers between devices with their start and end apart: 8 -> 0, of which waited for: 4 -> 0; matrix products, arithmetic and copies ran while one was open for 22% -> 0% of each run, Pallas kernels for 0% -> 0%
where the time goes in v1:
time: 38.1 us; the launch traced here: 37.5 us
  Pallas kernels  25.3 us (66%)
  local copies, waits for them, and re-layouts  12.1 us (32%)
    pallas_call x1, Pallas kernels, one_kernel(): pl.pallas_call(functools.partial(mixer_kernel, blocks, groups), out_shape...  25.3 us
    unnamed x25, local copies, waits for them, and re-layouts  12.1 us

profile of v1, /device:TPU:0, one launch (start us, length us, event | category | flops | bytes accessed | tf_op | source)
XLA Modules:
  0.0 37.5 jit_solution(1927957241266179348)
XLA Ops:
  0.0 0.0 copy-start
  0.0 1.9 %copy-done = bf16[1024,1536]{1,0:T(8,128)(2,1)S(1)} copy-done((bf16[1024,1536]{1,0:T(8,128)(2,1)S(1)}, bf16[1024,1536]{1,0:T(8,128)(2,1)}, u32[]{:S(2)}) %copy-start) | copy-done | bytes 3145752
  1.9 0.0 copy-start.1
  1.9 1.2 %copy-done.1 = bf16[512,1024]{1,0:T(8,128)(2,1)S(1)} copy-done((bf16[512,1024]{1,0:T(8,128)(2,1)S(1)}, bf16[512,1024]{1,0:T(8,128)(2,1)}, u32[]{:S(2)}) %copy-start.1) | copy-done | bytes 1048600
  3.1 0.0 copy-start.2
  3.1 0.9 %copy-done.2 = bf16[128,1024]{1,0:T(8,128)(2,1)S(1)} copy-done((bf16[128,1024]{1,0:T(8,128)(2,1)S(1)}, bf16[128,1024]{1,0:T(8,128)(2,1)}, u32[]{:S(2)}) %copy-start.2) | copy-done | bytes 262168
  4.1 0.0 copy-start.3
  4.1 0.9 %copy-done.3 = bf16[2,256,256]{2,1,0:T(8,128)(2,1)S(1)} copy-done((bf16[2,256,256]{2,1,0:T(8,128)(2,1)S(1)}, bf16[2,256,256]{2,1,0:T(8,128)(2,1)}, u32[]{:S(2)}) %copy-start.3) | copy-done | bytes 262168
  5.0 0.0 copy-start.4
  5.0 0.9 %copy-done.4 = bf16[2,256,256]{2,1,0:T(8,128)(2,1)S(1)} copy-done((bf16[2,256,256]{2,1,0:T(8,128)(2,1)S(1)}, bf16[2,256,256]{2,1,0:T(8,128)(2,1)}, u32[]{:S(2)}) %copy-start.4) | copy-done | bytes 262168
  6.0 0.0 copy-start.5
  6.0 0.9 %copy-done.5 = bf16[128,512]{1,0:T(8,128)(2,1)S(1)} copy-done((bf16[128,512]{1,0:T(8,128)(2,1)S(1)}, bf16[128,512]{1,0:T(8,128)(2,1)}, u32[]{:S(2)}) %copy-start.5) | copy-done | bytes 131096
  6.9 0.0 copy-start.6
  6.9 0.9 %copy-done.6 = bf16[128,512]{1,0:T(8,128)(2,1)S(1)} copy-done((bf16[128,512]{1,0:T(8,128)(2,1)S(1)}, bf16[128,512]{1,0:T(8,128)(2,1)}, u32[]{:S(2)}) %copy-start.6) | copy-done | bytes 131096
  7.8 0.0 copy-start.7
  7.8 0.8 %copy-done.7 = f32[2,32,128]{2,1,0:T(8,128)S(1)} copy-done((f32[2,32,128]{2,1,0:T(8,128)S(1)}, f32[2,32,128]{2,1,0:T(8,128)}, u32[]{:S(2)}) %copy-start.7) | copy-done | bytes 32792
  8.5 0.0 copy-start.8
  8.5 0.8 %copy-done.8 = bf16[128,64]{1,0:T(8,128)(2,1)S(1)} copy-done((bf16[128,64]{1,0:T(8,128)(2,1)S(1)}, bf16[128,64]{1,0:T(8,128)(2,1)}, u32[]{:S(2)}) %copy-start.8) | copy-done | bytes 16408
  9.3 0.0 copy-start.9
  9.3 0.7 %copy-done.9 = f32[3,1536]{1,0:T(4,128)S(1)} copy-done((f32[3,1536]{1,0:T(4,128)S(1)}, f32[3,1536]{1,0:T(4,128)}, u32[]{:S(2)}) %copy-start.9) | copy-done | bytes 18456
  10.0 0.0 copy-start.10
  10.0 0.7 %copy-done.10 = bf16[64,64]{1,0:T(8,128)(2,1)S(1)} copy-done((bf16[64,64]{1,0:T(8,128)(2,1)S(1)}, bf16[64,64]{1,0:T(8,128)(2,1)}, u32[]{:S(2)}) %copy-start.10) | copy-done | bytes 8216
  10.7 0.0 copy-start.11
  10.8 0.7 %copy-done.11 = f32[512]{0:T(512)S(1)} copy-done((f32[512]{0:T(512)S(1)}, f32[512]{0:T(512)}, u32[]{:S(2)}) %copy-start.11) | copy-done | bytes 2072
  11.4 25.3 %shard_map.118 = bf16[128,1024]{1,0:T(8,128)(2,1)S(1)} custom-call(bf16[128,1024]{1,0:T(8,128)(2,1)S(1)} %copy-done.2, bf16[128,512]{1,0:T(8,128)(2,1)S(1)} %copy-done.5, bf16[128,512]{1,0:T(8,128)(2,1)S(1)} %copy-done.6, f32[3,1536]{1,0:T(4,128)S(1)} %copy-done.9, f32[1,512]{1,0:T(1,128)S(1)} %bitcast.1, bf16[128,64]{1,0:T(8,128)(2,1)S(1)} %copy-done.8, ...), custom_call_target="tpu_custom_call" | custom-call | tf_op jit(solution)/shard_map/pallas_call | solution.py:431
  36.8 0.7 %copy.14 = bf16[128,1024]{1,0:T(8,128)(2,1)} copy(bf16[128,1024]{1,0:T(8,128)(2,1)S(1)} %shard_map.118) | data formatting | bytes 524288
Async XLA Ops:
  0.0 1.9 %copy-start = (bf16[1024,1536]{1,0:T(8,128)(2,1)S(1)}, bf16[1024,1536]{1,0:T(8,128)(2,1)}, u32[]{:S(2)}) copy-start(bf16[1024,1536]{1,0:T(8,128)(2,1)} %w_in_hbm.1) | copy-start | bytes 9437188
  1.9 1.2 %copy-start.1 = (bf16[512,1024]{1,0:T(8,128)(2,1)S(1)}, bf16[512,1024]{1,0:T(8,128)(2,1)}, u32[]{:S(2)}) copy-start(bf16[512,1024]{1,0:T(8,128)(2,1)} %w_out_hbm.1) | copy-start | bytes 3145732
  3.1 0.9 %copy-start.2 = (bf16[128,1024]{1,0:T(8,128)(2,1)S(1)}, bf16[128,1024]{1,0:T(8,128)(2,1)}, u32[]{:S(2)}) copy-start(bf16[128,1024]{1,0:T(8,128)(2,1)} %tokens.1) | copy-start | bytes 786436
  4.1 0.9 %copy-start.3 = (bf16[2,256,256]{2,1,0:T(8,128)(2,1)S(1)}, bf16[2,256,256]{2,1,0:T(8,128)(2,1)}, u32[]{:S(2)}) copy-start(bf16[2,256,256]{2,1,0:T(8,128)(2,1)} %constant.14.clone.within_back_hbm) | copy-start | bytes 786436
  5.0 0.9 %copy-start.4 = (bf16[2,256,256]{2,1,0:T(8,128)(2,1)S(1)}, bf16[2,256,256]{2,1,0:T(8,128)(2,1)}, u32[]{:S(2)}) copy-start(bf16[2,256,256]{2,1,0:T(8,128)(2,1)} %constant.13.clone.within_hbm) | copy-start | bytes 786436
  6.0 0.9 %copy-start.5 = (bf16[128,512]{1,0:T(8,128)(2,1)S(1)}, bf16[128,512]{1,0:T(8,128)(2,1)}, u32[]{:S(2)}) copy-start(bf16[128,512]{1,0:T(8,128)(2,1)} %causal.1) | copy-start | bytes 393220
  6.9 0.9 %copy-start.6 = (bf16[128,512]{1,0:T(8,128)(2,1)S(1)}, bf16[128,512]{1,0:T(8,128)(2,1)}, u32[]{:S(2)}) copy-start(bf16[128,512]{1,0:T(8,128)(2,1)} %anti.1) | copy-start | bytes 393220
  7.8 0.8 %copy-start.7 = (f32[2,32,128]{2,1,0:T(8,128)S(1)}, f32[2,32,128]{2,1,0:T(8,128)}, u32[]{:S(2)}) copy-start(f32[2,32,128]{2,1,0:T(8,128)} %constant.11.clone.twist) | copy-start | bytes 98308
  8.5 0.8 %copy-start.8 = (bf16[128,64]{1,0:T(8,128)(2,1)S(1)}, bf16[128,64]{1,0:T(8,128)(2,1)}, u32[]{:S(2)}) copy-start(bf16[128,64]{1,0:T(8,128)(2,1)} %constant.10.clone.across) | copy-start | bytes 49156
  9.3 0.7 %copy-start.9 = (f32[3,1536]{1,0:T(4,128)S(1)}, f32[3,1536]{1,0:T(4,128)}, u32[]{:S(2)}) copy-start(f32[3,1536]{1,0:T(4,128)} %conv_taps.1) | copy-start | bytes 55300
  10.0 0.7 %copy-start.10 = (bf16[64,64]{1,0:T(8,128)(2,1)S(1)}, bf16[64,64]{1,0:T(8,128)(2,1)}, u32[]{:S(2)}) copy-start(bf16[64,64]{1,0:T(8,128)(2,1)} %constant.12.clone.back) | copy-start | bytes 24580
  10.7 0.7 %copy-start.11 = (f32[512]{0:T(512)S(1)}, f32[512]{0:T(512)}, u32[]{:S(2)}) copy-start(f32[512]{0:T(512)} %param.17) | copy-start | bytes 6148

commit v2 on v1

--- a/solution.py
+++ b/solution.py
@@ -172,12 +172,11 @@
     twist = np.stack([np.cos(turn), np.sin(turn)]).astype(np.float32)
     grid = np.outer(np.arange(width), np.arange(width)) % width * (2.0 * np.pi / width)
     cos, sin = np.cos(grid), np.sin(grid)
-    within = np.stack(split(np.block([[cos, -sin], [sin, cos]])))
-    within_back = np.stack(split(np.block([[cos, sin], [-sin, cos]])))
+    within = np.block([[cos, -sin], [sin, cos]]).astype(np.float32)
     back = rows[:, :blocks].T
-    back = np.concatenate([np.cos(back), -np.sin(back)], axis=1) * (2.0 / length)
+    back = np.concatenate([np.cos(back), np.sin(back)], axis=1) * (2.0 / length)
     back = np.concatenate(split(back), axis=0)
-    return across, twist, within, within_back, back
+    return across, twist, within, back
 
 
 def dot32(a, b):
@@ -193,7 +192,18 @@
 def mixer_kernel(
     blocks,
     groups,
-    tokens,
+    tokens_hbm,
+    causal_hbm,
+    anti_hbm,
+    conv_taps_hbm,
+    skip_gain_hbm,
+    across_hbm,
+    twist_hbm,
+    back_hbm,
+    w_in_hbm,
+    w_out_hbm,
+    within_hbm,
+    out,
     causal,
     anti,
     conv_taps,
@@ -201,15 +211,10 @@
     across,
     twist,
     back,
-    w_in_hbm,
-    w_out_hbm,
-    within_hbm,
-    within_back_hbm,
-    out,
     w_in,
     w_out,
+    within_whole,
     within,
-    within_back,
     framed,
     edge_out,
     edge_in,
@@ -232,9 +237,10 @@
     ret_recv,
 ):
     f32, bf16 = jnp.float32, jnp.bfloat16
-    width, depth = tokens.shape
+    width, depth = tokens_hbm.shape
     channels = w_out.shape[0]
     mine = channels // blocks
+    tokens = framed.at[0:width]
     me = lax.axis_index("blk") * groups + lax.axis_index("fft")
 
     def place(peer):
@@ -244,10 +250,17 @@
         pltpu.make_async_copy(src, dst, load_sem.at[i])
         for i, (src, dst) in enumerate(
             (
+                (causal_hbm, causal),
+                (anti_hbm, anti),
+                (tokens_hbm, tokens),
                 (w_in_hbm, w_in),
-                (within_hbm, within),
-                (within_back_hbm, within_back),
+                (conv_taps_hbm, conv_taps),
+                (across_hbm, across),
+                (twist_hbm, twist),
+                (within_hbm, within_whole),
+                (back_hbm, back),
                 (w_out_hbm, w_out),
+                (skip_gain_hbm, skip_gain),
             )
         )
     ]
@@ -284,6 +297,8 @@
         most = src.at[pl.ds(0, blocks - 1)]
         pltpu.make_async_copy(most, most, send_sem).wait()
 
+    for load in loads[:3]:
+        load.wait()
     edge_out[0] = tokens[width - 16 :, :].astype(f32)[15:16]
     edge_out[1] = tokens[0:16, :].astype(f32)[0:1]
     filt_out[:, 0:mine, :] = (
@@ -311,8 +326,6 @@
         edge.start()
     send_all(filt_out, filt_in, filt_send, filt_recv)
 
-    framed[0:width, :] = tokens[...]
-    loads[0].wait()
     for edge in edges:
         edge.wait()
     row16 = lax.broadcasted_iota(jnp.int32, (16, depth), 0)
@@ -322,6 +335,8 @@
         row16 == 0, prev, jnp.where(row16 == 1, following, 0.0)
     ).astype(bf16)
 
+    for load in loads[3:5]:
+        load.wait()
     row = lax.broadcasted_iota(jnp.int32, (width, channels), 0)
 
     def stream(part):
@@ -340,28 +355,30 @@
     send_all(sig_out, sig_in, sig_send, sig_recv)
     second = stream(1)
 
+    for load in loads[5:9]:
+        load.wait()
+    within[0], within[1] = halves(within_whole[...])
     cos, sin = twist[0], twist[1]
 
     def lane(x, c):
         return x[:, c * width : (c + 1) * width]
 
-    def times(x, mats):
+    def twisted(real, imag):
+        return [real * cos + imag * sin, imag * cos - real * sin]
+
+    def along(x):
         high, low = halves(x)
-        return dot32(high, mats[0]) + dot32(low, mats[0]) + dot32(high, mats[1])
+        return dot32(high, within[0]) + dot32(low, within[0]) + dot32(high, within[1])
 
     def forward(grid, mats):
         both = dot32(mats, grid)
         freq = both[: 2 * blocks] + both[2 * blocks :]
         parts = []
         for c in range(mine):
-            real, imag = lane(freq[:blocks], c), lane(freq[blocks:], c)
-            parts.append(
-                jnp.concatenate([real * cos + imag * sin, imag * cos - real * sin], axis=1)
-            )
-        return times(jnp.concatenate(parts, axis=0), within)
-
-    loads[1].wait()
-    loads[2].wait()
+            pair = twisted(lane(freq[:blocks], c), lane(freq[blocks:], c))
+            parts.append(jnp.concatenate(pair, axis=1))
+        return along(jnp.concatenate(parts, axis=0))
+
     arrived(filt_in, filt_recv)
     spread[...] = filt_in[...].astype(f32).reshape(2 * blocks * mine, width)
     grid = jnp.concatenate(
@@ -388,16 +405,13 @@
     s_real, s_imag = sig[:, :width], sig[:, width:]
     f_real, f_imag = spectrum[:, :width], spectrum[:, width:]
     product = jnp.concatenate(
-        [s_real * f_real - s_imag * f_imag, s_real * f_imag + s_imag * f_real], axis=1
-    )
-    turned = times(product, within_back)
+        [s_real * f_real - s_imag * f_imag, -(s_real * f_imag + s_imag * f_real)], axis=1
+    )
+    turned = along(product)
     parts = []
     for c in range(mine):
         rows = turned[c * blocks : (c + 1) * blocks]
-        real, imag = rows[:, :width], rows[:, width:]
-        parts.append(
-            jnp.concatenate([real * cos - imag * sin, imag * cos + real * sin], axis=0)
-        )
+        parts.append(jnp.concatenate(twisted(rows[:, :width], rows[:, width:]), axis=0))
     high, low = halves(jnp.concatenate(parts, axis=1))
     both = dot32(back[...], high)
     conv = both[:blocks] + both[blocks:] + dot32(back[0:blocks, :], low)
@@ -406,8 +420,9 @@
     ret_out[...] = spread[0 : blocks * mine, :].astype(bf16).reshape(blocks, mine, width)
     send_all(ret_out, ret_in, ret_send, ret_recv)
 
+    for load in loads[9:]:
+        load.wait()
     direct = skip_gain[...] * signal
-    loads[3].wait()
     arrived(ret_in, ret_recv)
     convolved = ret_in[...].astype(f32).reshape(channels, width).T + direct
     gated = (second * convolved).astype(bf16)
@@ -423,7 +438,7 @@
     groups = lax.axis_size("fft")
     blocks = lax.axis_size("blk") * groups
     mine = channels // blocks
-    across, twist, within, within_back, back = grid_constants(blocks, width)
+    across, twist, within, back = grid_constants(blocks, width)
     f32, bf16 = jnp.float32, jnp.bfloat16
     vmem = pl.BlockSpec(memory_space=pltpu.VMEM)
     whole = pl.BlockSpec(memory_space=pl.ANY)
@@ -431,13 +446,20 @@
     return pl.pallas_call(
         functools.partial(mixer_kernel, blocks, groups),
         out_shape=jax.ShapeDtypeStruct((width, w_out.shape[1]), bf16),
-        in_specs=[vmem] * 8 + [whole] * 4,
+        in_specs=[whole] * 11,
         out_specs=vmem,
         scratch_shapes=[
+            pltpu.VMEM(causal_taps.shape, bf16),
+            pltpu.VMEM(anticausal_taps.shape, bf16),
+            pltpu.VMEM(conv_taps.shape, f32),
+            pltpu.VMEM((1, channels), f32),
+            pltpu.VMEM(across.shape, bf16),
+            pltpu.VMEM(twist.shape, f32),
+            pltpu.VMEM(back.shape, bf16),
             pltpu.VMEM(w_in.shape, bf16),
             pltpu.VMEM(w_out.shape, bf16),
-            pltpu.VMEM(within.shape, bf16),
-            pltpu.VMEM(within_back.shape, bf16),
+            pltpu.VMEM(within.shape, f32),
+            pltpu.VMEM((2,) + within.shape, bf16),
             pltpu.VMEM((width + 16, depth), bf16),
             pltpu.VMEM((2, 1, depth), f32),
             pltpu.VMEM((2, 1, depth), f32),
@@ -449,7 +471,7 @@
             pltpu.VMEM((blocks, mine, width), bf16),
             pltpu.VMEM((2 * blocks * mine, width), f32),
             pltpu.VMEM((blocks * mine, 2 * width), f32),
-            one((4,)),
+            one((11,)),
             one((2,)),
             one((2,)),
             one,
@@ -460,7 +482,7 @@
             one,
         ],
         compiler_params=pltpu.CompilerParams(
-            collective_id=0, has_side_effects=True, vmem_limit_bytes=48 * 2**20
+            collective_id=0, has_side_effects=True, vmem_limit_bytes=63 * 2**20
         ),
     )(
         tokens,
@@ -474,7 +496,6 @@
         w_in,
         w_out,
         jnp.asarray(within),
-        jnp.asarray(within_back),
     )
 
 

time: 38.1 us -> 27.6 us (0.72); the launches traced: 37.5 us -> 27.5 us
  local copies, waits for them, and re-layouts: 12.1 us -> 1.67 us
  Pallas kernels: 25.3 us -> 25.8 us
    unnamed x25 -> x1, local copies, waits for them, and re-layouts: 12.1 us -> 1.67 us
    pallas_call x1, Pallas kernels: 25.3 us -> 25.8 us  [one_kernel(): pl.pallas_call(functools.partial(mixer_kernel, blocks, groups), out_shape...]
where the time goes in v2:
time: 27.6 us; the launch traced here: 27.5 us
  Pallas kernels  25.8 us (93%)
  local copies, waits for them, and re-layouts  1.67 us (6%)
    pallas_call x1, Pallas kernels, one_kernel(): pl.pallas_call(functools.partial(mixer_kernel, blocks, groups), out_shape...  25.8 us
    unnamed x1, local copies, waits for them, and re-layouts  1.67 us

profile of v2, /device:TPU:0, one launch (start us, length us, event | category | flops | bytes accessed | tf_op | source)
XLA Modules:
  0.0 27.5 jit_solution(11249465317834024864)
XLA Ops:
  0.0 25.8 %shard_map.109 = bf16[128,1024]{1,0:T(8,128)(2,1)} custom-call(bf16[128,1024]{1,0:T(8,128)(2,1)} %tokens_hbm.1, bf16[128,512]{1,0:T(8,128)(2,1)} %causal_hbm.1, bf16[128,512]{1,0:T(8,128)(2,1)} %anti_hbm.1, f32[3,1536]{1,0:T(4,128)} %conv_taps_hbm.1, f32[1,512]{1,0:T(1,128)} %bitcast.1, bf16[128,64]{1,0:T(8,128)(2,1)} %constant.8.clone.across_hbm, ...), custom_call_target="tpu_custom_call" | custom-call | tf_op jit(solution)/shard_map/pallas_call | solution.py:446
  25.8 1.7 %copy.13 = bf16[128,1024]{1,0:T(8,128)(2,1)} copy(bf16[128,1024]{1,0:T(8,128)(2,1)} %shard_map.109) | data formatting | bytes 524288

commit v3 on v2

--- a/solution.py
+++ b/solution.py
@@ -241,10 +241,20 @@
     channels = w_out.shape[0]
     mine = channels // blocks
     tokens = framed.at[0:width]
-    me = lax.axis_index("blk") * groups + lax.axis_index("fft")
-
-    def place(peer):
-        return (peer // groups, peer % groups)
+    blk, fft = lax.axis_index("blk"), lax.axis_index("fft")
+    me = blk * groups + fft
+    levels = blocks // groups
+    peers = []
+    for turn in range(levels - 1, -1, -1):
+        level = blk ^ turn
+        for step in range(groups):
+            if turn > 0 or step > 0:
+                other = (fft + step) & (groups - 1)
+                peers.append((level * groups + other, (level, other)))
+
+    barrier = pltpu.get_barrier_semaphore()
+    for _, coords in peers:
+        pl.semaphore_signal(barrier, inc=1, device_id=coords, device_id_type=MESH)
 
     loads = [
         pltpu.make_async_copy(src, dst, load_sem.at[i])
@@ -267,24 +277,14 @@
     for load in loads:
         load.start()
 
-    barrier = pltpu.get_barrier_semaphore()
-
-    @pl.loop(1, blocks)
-    def _(i):
-        pl.semaphore_signal(
-            barrier, inc=1, device_id=place((me + i) % blocks), device_id_type=MESH
-        )
-
     def send_all(src, dst, send_sem, recv_sem):
-        @pl.loop(1, blocks)
-        def _(i):
-            peer = (me + i) % blocks
+        for peer, coords in peers:
             pltpu.make_async_remote_copy(
                 src_ref=src.at[peer],
                 dst_ref=dst.at[me],
                 send_sem=send_sem,
                 recv_sem=recv_sem,
-                device_id=place(peer),
+                device_id=coords,
                 device_id_type=MESH,
             ).start()
 
@@ -317,10 +317,10 @@
             dst_ref=edge_in.at[i],
             send_sem=edge_send.at[i],
             recv_sem=edge_recv.at[i],
-            device_id=place((me + step) % blocks),
+            device_id=(at // groups, at % groups),
             device_id_type=MESH,
         )
-        for i, step in ((0, 1), (1, blocks - 1))
+        for i, at in enumerate(((me + 1) % blocks, (me + blocks - 1) % blocks))
     ]
     for edge in edges:
         edge.start()
@@ -441,12 +441,12 @@
     across, twist, within, back = grid_constants(blocks, width)
     f32, bf16 = jnp.float32, jnp.bfloat16
     vmem = pl.BlockSpec(memory_space=pltpu.VMEM)
-    whole = pl.BlockSpec(memory_space=pl.ANY)
+    hbm = pl.BlockSpec(memory_space=pl.ANY)
     one = pltpu.SemaphoreType.DMA
     return pl.pallas_call(
         functools.partial(mixer_kernel, blocks, groups),
         out_shape=jax.ShapeDtypeStruct((width, w_out.shape[1]), bf16),
-        in_specs=[whole] * 11,
+        in_specs=[hbm] * 11,
         out_specs=vmem,
         scratch_shapes=[
             pltpu.VMEM(causal_taps.shape, bf16),

time: 27.6 us -> 27.5 us (level)
  no operation moved by 1% of the time
where the time goes in v3:
time: 27.5 us; the launch traced here: 27.4 us
  Pallas kernels  25.7 us (93%)
  local copies, waits for them, and re-layouts  1.67 us (6%)
    pallas_call x1, Pallas kernels, one_kernel(): pl.pallas_call(functools.partial(mixer_kernel, blocks, groups), out_shape...  25.7 us
    unnamed x1, local copies, waits for them, and re-layouts  1.67 us

profile of v3, /device:TPU:0, one launch (start us, length us, event | category | flops | bytes accessed | tf_op | source)
XLA Modules:
  0.0 27.4 jit_solution(4897287106533794363)
XLA Ops:
  0.0 25.7 %shard_map.109 = bf16[128,1024]{1,0:T(8,128)(2,1)} custom-call(bf16[128,1024]{1,0:T(8,128)(2,1)} %tokens_hbm.1, bf16[128,512]{1,0:T(8,128)(2,1)} %causal_hbm.1, bf16[128,512]{1,0:T(8,128)(2,1)} %anti_hbm.1, f32[3,1536]{1,0:T(4,128)} %conv_taps_hbm.1, f32[1,512]{1,0:T(1,128)} %bitcast.1, bf16[128,64]{1,0:T(8,128)(2,1)} %constant.8.clone.across_hbm, ...), custom_call_target="tpu_custom_call" | custom-call | tf_op jit(solution)/shard_map/pallas_call | solution.py:446
  25.7 1.7 %copy.13 = bf16[128,1024]{1,0:T(8,128)(2,1)} copy(bf16[128,1024]{1,0:T(8,128)(2,1)} %shard_map.109) | data formatting | bytes 524288

commit v4 on v3

--- a/solution.py
+++ b/solution.py
@@ -357,7 +357,7 @@
 
     for load in loads[5:9]:
         load.wait()
-    within[0], within[1] = halves(within_whole[...])
+    within[0] = within_whole[...].astype(bf16)
     cos, sin = twist[0], twist[1]
 
     def lane(x, c):
@@ -367,12 +367,10 @@
         return [real * cos + imag * sin, imag * cos - real * sin]
 
     def along(x):
-        high, low = halves(x)
-        return dot32(high, within[0]) + dot32(low, within[0]) + dot32(high, within[1])
+        return dot32(x.astype(bf16), within[0])
 
     def forward(grid, mats):
-        both = dot32(mats, grid)
-        freq = both[: 2 * blocks] + both[2 * blocks :]
+        freq = dot32(mats[: 2 * blocks], grid)
         parts = []
         for c in range(mine):
             pair = twisted(lane(freq[:blocks], c), lane(freq[blocks:], c))
@@ -412,9 +410,7 @@
     for c in range(mine):
         rows = turned[c * blocks : (c + 1) * blocks]
         parts.append(jnp.concatenate(twisted(rows[:, :width], rows[:, width:]), axis=0))
-    high, low = halves(jnp.concatenate(parts, axis=1))
-    both = dot32(back[...], high)
-    conv = both[:blocks] + both[blocks:] + dot32(back[0:blocks, :], low)
+    conv = dot32(back[0:blocks, :], jnp.concatenate(parts, axis=1).astype(bf16))
     for c in range(mine):
         spread[pl.ds(c, blocks, stride=mine), :] = lane(conv, c)
     ret_out[...] = spread[0 : blocks * mine, :].astype(bf16).reshape(blocks, mine, width)
@@ -445,7 +441,7 @@
     one = pltpu.SemaphoreType.DMA
     return pl.pallas_call(
         functools.partial(mixer_kernel, blocks, groups),
-        out_shape=jax.ShapeDtypeStruct((width, w_out.shape[1]), bf16),
+        out_shape=pltpu.VMEM((width, w_out.shape[1]), bf16),
         in_specs=[hbm] * 11,
         out_specs=vmem,
         scratch_shapes=[
@@ -482,7 +478,7 @@
             one,
         ],
         compiler_params=pltpu.CompilerParams(
-            collective_id=0, has_side_effects=True, vmem_limit_bytes=63 * 2**20
+            collective_id=0, has_side_effects=True, vmem_limit_bytes=62 * 2**20
         ),
     )(
         tokens,

time: 27.5 us -> 25 us (0.909)
  Pallas kernels: 25.7 us -> 24.2 us
  local copies, waits for them, and re-layouts: 1.67 us -> 0.71 us
    pallas_call x1, Pallas kernels: 25.7 us -> 24.2 us  [one_kernel(): pl.pallas_call(functools.partial(mixer_kernel, blocks, groups), out_shape...]
    unnamed x1, local copies, waits for them, and re-layouts: 1.67 us -> 0.71 us
where the time goes in v4:
time: 25 us; the launch traced here: 24.9 us
  Pallas kernels  24.2 us (97%)
  local copies, waits for them, and re-layouts  0.71 us (3%)
    pallas_call x1, Pallas kernels, one_kernel(): pl.pallas_call(functools.partial(mixer_kernel, blocks, groups), out_shape...  24.2 us
    unnamed x1, local copies, waits for them, and re-layouts  0.71 us

profile of v4, /device:TPU:0, one launch (start us, length us, event | category | flops | bytes accessed | tf_op | source)
XLA Modules:
  0.0 24.9 jit_solution(17600256020703208661)
XLA Ops:
  0.0 24.2 %shard_map.109 = bf16[128,1024]{1,0:T(8,128)(2,1)S(1)} custom-call(bf16[128,1024]{1,0:T(8,128)(2,1)} %tokens_hbm.1, bf16[128,512]{1,0:T(8,128)(2,1)} %causal_hbm.1, bf16[128,512]{1,0:T(8,128)(2,1)} %anti_hbm.1, f32[3,1536]{1,0:T(4,128)} %conv_taps_hbm.1, f32[1,512]{1,0:T(1,128)} %bitcast.1, bf16[128,64]{1,0:T(8,128)(2,1)} %constant.8.clone.across_hbm, ...), custom_call_target="tpu_custom_call" | custom-call | tf_op jit(solution)/shard_map/pallas_call | solution.py:442
  24.2 0.7 %copy.13 = bf16[128,1024]{1,0:T(8,128)(2,1)} copy(bf16[128,1024]{1,0:T(8,128)(2,1)S(1)} %shard_map.109) | data formatting | bytes 524288

commit v5 on v4

--- a/solution.py
+++ b/solution.py
@@ -159,15 +159,10 @@
     length = 2 * blocks * width
     half_freq = np.arange(blocks) + 0.5
 
-    def split(mat):
-        high = mat.astype(ml_dtypes.bfloat16)
-        low = (mat - high.astype(np.float64)).astype(ml_dtypes.bfloat16)
-        return high, low
-
     rows = np.outer(half_freq, np.arange(2 * blocks)) * (2.0 * np.pi / (2 * blocks))
     flip = np.where(np.arange(2 * blocks) < blocks, 1.0, -1.0)
     across = np.concatenate([np.cos(rows), -np.sin(rows)], axis=0) * flip
-    across = np.concatenate(split(across), axis=0)
+    across = across.astype(ml_dtypes.bfloat16)
     turn = np.outer(half_freq, np.arange(width)) * (2.0 * np.pi / length)
     twist = np.stack([np.cos(turn), np.sin(turn)]).astype(np.float32)
     grid = np.outer(np.arange(width), np.arange(width)) % width * (2.0 * np.pi / width)
@@ -175,18 +170,12 @@
     within = np.block([[cos, -sin], [sin, cos]]).astype(np.float32)
     back = rows[:, :blocks].T
     back = np.concatenate([np.cos(back), np.sin(back)], axis=1) * (2.0 / length)
-    back = np.concatenate(split(back), axis=0)
+    back = back.astype(ml_dtypes.bfloat16)
     return across, twist, within, back
 
 
 def dot32(a, b):
     return jnp.dot(a, b, preferred_element_type=jnp.float32)
-
-
-def halves(x):
-    high = x.astype(jnp.bfloat16)
-    low = (x - high.astype(jnp.float32)).astype(jnp.bfloat16)
-    return high, low
 
 
 def mixer_kernel(
@@ -225,7 +214,12 @@
     ret_out,
     ret_in,
     spread,
+    gather,
+    result,
     spectrum,
+    gate,
+    passed,
+    gated,
     load_sem,
     edge_send,
     edge_recv,
@@ -239,7 +233,7 @@
     f32, bf16 = jnp.float32, jnp.bfloat16
     width, depth = tokens_hbm.shape
     channels = w_out.shape[0]
-    mine = channels // blocks
+    parts, _, some, _ = sig_out.shape
     tokens = framed.at[0:width]
     blk, fft = lax.axis_index("blk"), lax.axis_index("fft")
     me = blk * groups + fft
@@ -250,10 +244,10 @@
         for step in range(groups):
             if turn > 0 or step > 0:
                 other = (fft + step) & (groups - 1)
-                peers.append((level * groups + other, (level, other)))
+                peers.append((turn, level * groups + other, (level, other)))
 
     barrier = pltpu.get_barrier_semaphore()
-    for _, coords in peers:
+    for _, _, coords in peers:
         pl.semaphore_signal(barrier, inc=1, device_id=coords, device_id_type=MESH)
 
     loads = [
@@ -278,38 +272,45 @@
         load.start()
 
     def send_all(src, dst, send_sem, recv_sem):
-        for peer, coords in peers:
+        for turn, peer, coords in peers:
             pltpu.make_async_remote_copy(
                 src_ref=src.at[peer],
                 dst_ref=dst.at[me],
                 send_sem=send_sem,
-                recv_sem=recv_sem,
+                recv_sem=recv_sem.at[turn],
                 device_id=coords,
                 device_id_type=MESH,
             ).start()
-
-        pltpu.make_async_copy(src.at[me], dst.at[me], recv_sem).start()
-
-    def arrived(dst, recv_sem):
-        pltpu.make_async_copy(dst, dst, recv_sem).wait()
+        pltpu.make_async_copy(src.at[me], dst.at[me], recv_sem.at[0]).start()
+
+    def plane_of(dst, turn):
+        return dst.at[pl.ds((blk ^ turn) * groups, groups)]
+
+    def arrived(dst, recv_sem, turn):
+        plane = plane_of(dst, turn)
+        pltpu.make_async_copy(plane, plane, recv_sem.at[turn]).wait()
+
+    def all_arrived(dst, recv_sem):
+        for turn in range(levels):
+            arrived(dst, recv_sem, turn)
 
     def sent(src, send_sem):
         most = src.at[pl.ds(0, blocks - 1)]
         pltpu.make_async_copy(most, most, send_sem).wait()
+
+    def chunks(x):
+        return x.T.reshape(blocks, parts, some, width)
 
     for load in loads[:3]:
         load.wait()
     edge_out[0] = tokens[width - 16 :, :].astype(f32)[15:16]
     edge_out[1] = tokens[0:16, :].astype(f32)[0:1]
-    filt_out[:, 0:mine, :] = (
-        causal[...].astype(f32).T.astype(bf16).reshape(blocks, mine, width)
-    )
     unused = (lax.broadcasted_iota(jnp.int32, anti.shape, 0) == 0) & (me == 0)
-    filt_out[:, mine:, :] = (
-        jnp.where(unused, 0.0, anti[...].astype(f32))
-        .T.astype(bf16)
-        .reshape(blocks, mine, width)
-    )
+    causal_rows = chunks(causal[...].astype(f32))
+    anti_rows = chunks(jnp.where(unused, 0.0, anti[...].astype(f32)))
+    for part in range(parts):
+        filt_out[part, :, 0:some, :] = causal_rows[:, part].astype(bf16)
+        filt_out[part, :, some:, :] = anti_rows[:, part].astype(bf16)
     pl.semaphore_wait(barrier, blocks - 1)
     edges = [
         pltpu.make_async_remote_copy(
@@ -324,8 +325,18 @@
     ]
     for edge in edges:
         edge.start()
-    send_all(filt_out, filt_in, filt_send, filt_recv)
-
+
+    def send_part(bufs, part):
+        src, dst, send_sem, recv_sem = bufs
+        send_all(src.at[part], dst.at[part], send_sem.at[part], recv_sem.at[part])
+
+    filt = (filt_out, filt_in, filt_send, filt_recv)
+    sig = (sig_out, sig_in, sig_send, sig_recv)
+    ret = (ret_out, ret_in, ret_send, ret_recv)
+    send_part(filt, 0)
+
+    for load in loads[3:5]:
+        load.wait()
     for edge in edges:
         edge.wait()
     row16 = lax.broadcasted_iota(jnp.int32, (16, depth), 0)
@@ -334,13 +345,10 @@
     framed[width:, :] = jnp.where(
         row16 == 0, prev, jnp.where(row16 == 1, following, 0.0)
     ).astype(bf16)
-
-    for load in loads[3:5]:
-        load.wait()
     row = lax.broadcasted_iota(jnp.int32, (width, channels), 0)
 
-    def stream(part):
-        cols = slice(part * channels, (part + 1) * channels)
+    def stream(which):
+        cols = slice(which * channels, (which + 1) * channels)
         proj = dot32(framed[...], w_in[:, cols]).astype(bf16).astype(f32)
         here = proj[:width]
         before = jnp.where(row == 0, proj[width : width + 1], pltpu.roll(here, 1, 0))
@@ -351,81 +359,90 @@
         return taps[0:1] * before + taps[1:2] * here + taps[2:3] * after
 
     signal = stream(0) * stream(2)
-    sig_out[...] = signal.T.astype(bf16).reshape(blocks, mine, width)
-    send_all(sig_out, sig_in, sig_send, sig_recv)
+    signal_rows = chunks(signal)
+    for part in range(parts):
+        sig_out[part] = signal_rows[:, part].astype(bf16)
+        send_part(sig, part)
+        if part + 1 < parts:
+            send_part(filt, part + 1)
+
+    for load in loads[5:]:
+        load.wait()
     second = stream(1)
-
-    for load in loads[5:9]:
-        load.wait()
-    within[0] = within_whole[...].astype(bf16)
+    direct = second * (skip_gain[...] * signal)
+    span = channels // levels
+    for level in range(levels):
+        gate[level] = second[:, level * span : (level + 1) * span]
+        passed[level] = direct[:, level * span : (level + 1) * span]
+    within[...] = within_whole[...].astype(bf16)
     cos, sin = twist[0], twist[1]
+
+    def twisted(real, imag, axis):
+        return jnp.concatenate([real * cos + imag * sin, imag * cos - real * sin], axis=axis)
 
     def lane(x, c):
         return x[:, c * width : (c + 1) * width]
 
-    def twisted(real, imag):
-        return [real * cos + imag * sin, imag * cos - real * sin]
-
-    def along(x):
-        return dot32(x.astype(bf16), within[0])
-
-    def forward(grid, mats):
-        freq = dot32(mats[: 2 * blocks], grid)
-        parts = []
-        for c in range(mine):
-            pair = twisted(lane(freq[:blocks], c), lane(freq[blocks:], c))
-            parts.append(jnp.concatenate(pair, axis=1))
-        return along(jnp.concatenate(parts, axis=0))
-
-    arrived(filt_in, filt_recv)
-    spread[...] = filt_in[...].astype(f32).reshape(2 * blocks * mine, width)
-    grid = jnp.concatenate(
-        [
-            jnp.concatenate(
-                [
-                    spread[pl.ds(c, blocks, stride=2 * mine), :],
-                    spread[pl.ds(mine + c, blocks, stride=2 * mine), :],
-                ],
-                axis=0,
-            ).astype(bf16)
-            for c in range(mine)
-        ],
-        axis=1,
-    )
-    spectrum[...] = forward(grid, across[...])
-
-    arrived(sig_in, sig_recv)
-    spread[0 : blocks * mine, :] = sig_in[...].astype(f32).reshape(blocks * mine, width)
-    grid = jnp.concatenate(
-        [spread[pl.ds(c, blocks, stride=mine), :].astype(bf16) for c in range(mine)], axis=1
-    )
-    sig = forward(grid, across[:, 0:blocks])
-    s_real, s_imag = sig[:, :width], sig[:, width:]
-    f_real, f_imag = spectrum[:, :width], spectrum[:, width:]
-    product = jnp.concatenate(
-        [s_real * f_real - s_imag * f_imag, -(s_real * f_imag + s_imag * f_real)], axis=1
-    )
-    turned = along(product)
-    parts = []
-    for c in range(mine):
-        rows = turned[c * blocks : (c + 1) * blocks]
-        parts.append(jnp.concatenate(twisted(rows[:, :width], rows[:, width:]), axis=0))
-    conv = dot32(back[0:blocks, :], jnp.concatenate(parts, axis=1).astype(bf16))
-    for c in range(mine):
-        spread[pl.ds(c, blocks, stride=mine), :] = lane(conv, c)
-    ret_out[...] = spread[0 : blocks * mine, :].astype(bf16).reshape(blocks, mine, width)
-    send_all(ret_out, ret_in, ret_send, ret_recv)
-
-    for load in loads[9:]:
-        load.wait()
-    direct = skip_gain[...] * signal
-    arrived(ret_in, ret_recv)
-    convolved = ret_in[...].astype(f32).reshape(channels, width).T + direct
-    gated = (second * convolved).astype(bf16)
-    out[...] = dot32(gated, w_out[...]).astype(bf16)
-    sent(filt_out, filt_send)
-    sent(sig_out, sig_send)
-    sent(ret_out, ret_send)
+    def forward(columns, mats):
+        freq = dot32(mats, jnp.concatenate(columns, axis=1))
+        turned = [
+            twisted(lane(freq[:blocks], c), lane(freq[blocks:], c), 1)
+            for c in range(len(columns))
+        ]
+        return dot32(jnp.concatenate(turned, axis=0).astype(bf16), within[...])
+
+    few = 4
+    sets = [list(range(c, c + few)) for c in range(0, some, few)]
+    for part in range(parts):
+        all_arrived(filt_in.at[part], filt_recv.at[part])
+        spread[...] = filt_in[part].astype(f32).reshape(2 * blocks * some, width)
+        for n, members in enumerate(sets):
+            columns = [
+                jnp.concatenate(
+                    [
+                        spread[pl.ds(c, blocks, stride=2 * some), :],
+                        spread[pl.ds(some + c, blocks, stride=2 * some), :],
+                    ],
+                    axis=0,
+                ).astype(bf16)
+                for c in members
+            ]
+            spectrum[n] = forward(columns, across[...])
+
+        all_arrived(sig_in.at[part], sig_recv.at[part])
+        gather[...] = sig_in[part].astype(f32).reshape(blocks * some, width)
+        for n, members in enumerate(sets):
+            columns = [
+                gather[pl.ds(c, blocks, stride=some), :].astype(bf16) for c in members
+            ]
+            freq = forward(columns, across[:, 0:blocks])
+            s_real, s_imag = freq[:, :width], freq[:, width:]
+            f_real, f_imag = spectrum[n, :, :width], spectrum[n, :, width:]
+            product = jnp.concatenate(
+                [s_real * f_real - s_imag * f_imag, -(s_real * f_imag + s_imag * f_real)],
+                axis=1,
+            )
+            turned = dot32(product.astype(bf16), within[...])
+            pieces = [turned[i * blocks : (i + 1) * blocks] for i in range(few)]
+            pieces = [twisted(x[:, :width], x[:, width:], 0) for x in pieces]
+            conv = dot32(back[...], jnp.concatenate(pieces, axis=1).astype(bf16))
+            for i, c in enumerate(members):
+                result[pl.ds(c, blocks, stride=some), :] = lane(conv, i)
+        ret_out[part] = result[...].astype(bf16).reshape(blocks, some, width)
+        send_part(ret, part)
+
+    for turn in range(levels):
+        level = blk ^ turn
+        for part in range(parts):
+            arrived(ret_in.at[part], ret_recv.at[part], turn)
+        landed = [plane_of(ret_in.at[part], turn)[...].astype(f32) for part in range(parts)]
+        landed = jnp.concatenate(landed, axis=1).reshape(span, width).T
+        cols = pl.ds(pl.multiple_of(level * span, span), span)
+        gated[:, cols] = (gate[level] * landed + passed[level]).astype(bf16)
+    out[...] = dot32(gated[...], w_out[...]).astype(bf16)
+    for src, _, send_sem, _ in (filt, sig, ret):
+        for part in range(parts):
+            sent(src.at[part], send_sem.at[part])
 
 
 def one_kernel(tokens, w_in, conv_taps, causal_taps, anticausal_taps, skip_gain, w_out):
@@ -433,7 +450,9 @@
     channels = w_out.shape[0]
     groups = lax.axis_size("fft")
     blocks = lax.axis_size("blk") * groups
-    mine = channels // blocks
+    levels = lax.axis_size("blk")
+    parts = 1
+    some = channels // blocks // parts
     across, twist, within, back = grid_constants(blocks, width)
     f32, bf16 = jnp.float32, jnp.bfloat16
     vmem = pl.BlockSpec(memory_space=pltpu.VMEM)
@@ -455,27 +474,32 @@
             pltpu.VMEM(w_in.shape, bf16),
             pltpu.VMEM(w_out.shape, bf16),
             pltpu.VMEM(within.shape, f32),
-            pltpu.VMEM((2,) + within.shape, bf16),
+            pltpu.VMEM(within.shape, bf16),
             pltpu.VMEM((width + 16, depth), bf16),
             pltpu.VMEM((2, 1, depth), f32),
             pltpu.VMEM((2, 1, depth), f32),
-            pltpu.VMEM((blocks, 2 * mine, width), bf16),
-            pltpu.VMEM((blocks, 2 * mine, width), bf16),
-            pltpu.VMEM((blocks, mine, width), bf16),
-            pltpu.VMEM((blocks, mine, width), bf16),
-            pltpu.VMEM((blocks, mine, width), bf16),
-            pltpu.VMEM((blocks, mine, width), bf16),
-            pltpu.VMEM((2 * blocks * mine, width), f32),
-            pltpu.VMEM((blocks * mine, 2 * width), f32),
+            pltpu.VMEM((parts, blocks, 2 * some, width), bf16),
+            pltpu.VMEM((parts, blocks, 2 * some, width), bf16),
+            pltpu.VMEM((parts, blocks, some, width), bf16),
+            pltpu.VMEM((parts, blocks, some, width), bf16),
+            pltpu.VMEM((parts, blocks, some, width), bf16),
+            pltpu.VMEM((parts, blocks, some, width), bf16),
+            pltpu.VMEM((2 * blocks * some, width), f32),
+            pltpu.VMEM((blocks * some, width), f32),
+            pltpu.VMEM((blocks * some, width), f32),
+            pltpu.VMEM((some // 4, 4 * blocks, 2 * width), f32),
+            pltpu.VMEM((levels, width, channels // levels), f32),
+            pltpu.VMEM((levels, width, channels // levels), f32),
+            pltpu.VMEM((width, channels), bf16),
             one((11,)),
             one((2,)),
             one((2,)),
-            one,
-            one,
-            one,
-            one,
-            one,
-            one,
+            one((parts,)),
+            one((parts, levels)),
+            one((parts,)),
+            one((parts, levels)),
+            one((parts,)),
+            one((parts, levels)),
         ],
         compiler_params=pltpu.CompilerParams(
             collective_id=0, has_side_effects=True, vmem_limit_bytes=62 * 2**20

time: 25 us -> 26.2 us (1.048)
  Pallas kernels: 24.2 us -> 25.3 us
    pallas_call x1, Pallas kernels: 24.2 us -> 25.3 us  [one_kernel(): pl.pallas_call(functools.partial(mixer_kernel, blocks, groups), out_shape...]
where the time goes in v5:
time: 26.2 us; the launch traced here: 26.1 us
  Pallas kernels  25.3 us (97%)
  local copies, waits for them, and re-layouts  0.71 us (3%)
    pallas_call x1, Pallas kernels, one_kernel(): pl.pallas_call(functools.partial(mixer_kernel, blocks, groups), out_shape...  25.3 us
    unnamed x1, local copies, waits for them, and re-layouts  0.71 us

profile of v5, /device:TPU:0, one launch (start us, length us, event | category | flops | bytes accessed | tf_op | source)
XLA Modules:
  0.0 26.1 jit_solution(12657158148831403039)
XLA Ops:
  0.0 25.3 %shard_map.109 = bf16[128,1024]{1,0:T(8,128)(2,1)S(1)} custom-call(bf16[128,1024]{1,0:T(8,128)(2,1)} %tokens_hbm.1, bf16[128,512]{1,0:T(8,128)(2,1)} %causal_hbm.1, bf16[128,512]{1,0:T(8,128)(2,1)} %anti_hbm.1, f32[3,1536]{1,0:T(4,128)} %conv_taps_hbm.1, f32[1,512]{1,0:T(1,128)} %bitcast.1, bf16[64,64]{1,0:T(8,128)(2,1)} %constant.8.clone.across_hbm, ...), custom_call_target="tpu_custom_call" | custom-call | tf_op jit(solution)/shard_map/pallas_call | solution.py:461
  25.4 0.7 %copy.13 = bf16[128,1024]{1,0:T(8,128)(2,1)} copy(bf16[128,1024]{1,0:T(8,128)(2,1)S(1)} %shard_map.109) | data formatting | bytes 524288

commit v6 on v5

--- a/solution.py
+++ b/solution.py
@@ -451,7 +451,7 @@
     groups = lax.axis_size("fft")
     blocks = lax.axis_size("blk") * groups
     levels = lax.axis_size("blk")
-    parts = 1
+    parts = 2
     some = channels // blocks // parts
     across, twist, within, back = grid_constants(blocks, width)
     f32, bf16 = jnp.float32, jnp.bfloat16

time: 26.2 us -> 25.3 us (0.966)
  Pallas kernels: 25.3 us -> 24.5 us
    pallas_call x1, Pallas kernels: 25.3 us -> 24.5 us  [one_kernel(): pl.pallas_call(functools.partial(mixer_kernel, blocks, groups), out_shape...]
where the time goes in v6:
time: 25.3 us; the launch traced here: 25.2 us
  Pallas kernels  24.5 us (97%)
  local copies, waits for them, and re-layouts  0.71 us (3%)
    pallas_call x1, Pallas kernels, one_kernel(): pl.pallas_call(functools.partial(mixer_kernel, blocks, groups), out_shape...  24.5 us
    unnamed x1, local copies, waits for them, and re-layouts  0.71 us

profile of v6, /device:TPU:0, one launch (start us, length us, event | category | flops | bytes accessed | tf_op | source)
XLA Modules:
  0.0 25.2 jit_solution(7466216768704810439)
XLA Ops:
  0.0 24.5 %shard_map.109 = bf16[128,1024]{1,0:T(8,128)(2,1)S(1)} custom-call(bf16[128,1024]{1,0:T(8,128)(2,1)} %tokens_hbm.1, bf16[128,512]{1,0:T(8,128)(2,1)} %causal_hbm.1, bf16[128,512]{1,0:T(8,128)(2,1)} %anti_hbm.1, f32[3,1536]{1,0:T(4,128)} %conv_taps_hbm.1, f32[1,512]{1,0:T(1,128)} %bitcast.1, bf16[64,64]{1,0:T(8,128)(2,1)} %constant.8.clone.across_hbm, ...), custom_call_target="tpu_custom_call" | custom-call | tf_op jit(solution)/shard_map/pallas_call | solution.py:461
  24.5 0.7 %copy.13 = bf16[128,1024]{1,0:T(8,128)(2,1)} copy(bf16[128,1024]{1,0:T(8,128)(2,1)S(1)} %shard_map.109) | data formatting | bytes 524288

commit v7 on v6

--- a/solution.py
+++ b/solution.py
@@ -391,43 +391,39 @@
         ]
         return dot32(jnp.concatenate(turned, axis=0).astype(bf16), within[...])
 
-    few = 4
-    sets = [list(range(c, c + few)) for c in range(0, some, few)]
     for part in range(parts):
         all_arrived(filt_in.at[part], filt_recv.at[part])
         spread[...] = filt_in[part].astype(f32).reshape(2 * blocks * some, width)
-        for n, members in enumerate(sets):
-            columns = [
-                jnp.concatenate(
-                    [
-                        spread[pl.ds(c, blocks, stride=2 * some), :],
-                        spread[pl.ds(some + c, blocks, stride=2 * some), :],
-                    ],
-                    axis=0,
-                ).astype(bf16)
-                for c in members
-            ]
-            spectrum[n] = forward(columns, across[...])
+        columns = [
+            jnp.concatenate(
+                [
+                    spread[pl.ds(c, blocks, stride=2 * some), :],
+                    spread[pl.ds(some + c, blocks, stride=2 * some), :],
+                ],
+                axis=0,
+            ).astype(bf16)
+            for c in range(some)
+        ]
+        spectrum[...] = forward(columns, across[...])
 
         all_arrived(sig_in.at[part], sig_recv.at[part])
         gather[...] = sig_in[part].astype(f32).reshape(blocks * some, width)
-        for n, members in enumerate(sets):
-            columns = [
-                gather[pl.ds(c, blocks, stride=some), :].astype(bf16) for c in members
-            ]
-            freq = forward(columns, across[:, 0:blocks])
-            s_real, s_imag = freq[:, :width], freq[:, width:]
-            f_real, f_imag = spectrum[n, :, :width], spectrum[n, :, width:]
-            product = jnp.concatenate(
-                [s_real * f_real - s_imag * f_imag, -(s_real * f_imag + s_imag * f_real)],
-                axis=1,
-            )
-            turned = dot32(product.astype(bf16), within[...])
-            pieces = [turned[i * blocks : (i + 1) * blocks] for i in range(few)]
-            pieces = [twisted(x[:, :width], x[:, width:], 0) for x in pieces]
-            conv = dot32(back[...], jnp.concatenate(pieces, axis=1).astype(bf16))
-            for i, c in enumerate(members):
-                result[pl.ds(c, blocks, stride=some), :] = lane(conv, i)
+        columns = [
+            gather[pl.ds(c, blocks, stride=some), :].astype(bf16) for c in range(some)
+        ]
+        freq = forward(columns, across[:, 0:blocks])
+        s_real, s_imag = freq[:, :width], freq[:, width:]
+        f_real, f_imag = spectrum[:, :width], spectrum[:, width:]
+        product = jnp.concatenate(
+            [s_real * f_real - s_imag * f_imag, -(s_real * f_imag + s_imag * f_real)],
+            axis=1,
+        )
+        turned = dot32(product.astype(bf16), within[...])
+        pieces = [turned[i * blocks : (i + 1) * blocks] for i in range(some)]
+        pieces = [twisted(x[:, :width], x[:, width:], 0) for x in pieces]
+        conv = dot32(back[...], jnp.concatenate(pieces, axis=1).astype(bf16))
+        for c in range(some):
+            result[pl.ds(c, blocks, stride=some), :] = lane(conv, c)
         ret_out[part] = result[...].astype(bf16).reshape(blocks, some, width)
         send_part(ret, part)
 
@@ -487,7 +483,7 @@
             pltpu.VMEM((2 * blocks * some, width), f32),
             pltpu.VMEM((blocks * some, width), f32),
             pltpu.VMEM((blocks * some, width), f32),
-            pltpu.VMEM((some // 4, 4 * blocks, 2 * width), f32),
+            pltpu.VMEM((some * blocks, 2 * width), f32),
             pltpu.VMEM((levels, width, channels // levels), f32),
             pltpu.VMEM((levels, width, channels // levels), f32),
             pltpu.VMEM((width, channels), bf16),

time: 25.3 us -> 24.9 us (0.984)
  Pallas kernels: 24.5 us -> 24.1 us
    pallas_call x1, Pallas kernels: 24.5 us -> 24.1 us  [one_kernel(): pl.pallas_call(functools.partial(mixer_kernel, blocks, groups), out_shape...]
where the time goes in v7:
time: 24.9 us; the launch traced here: 24.8 us
  Pallas kernels  24.1 us (97%)
  local copies, waits for them, and re-layouts  0.71 us (3%)
    pallas_call x1, Pallas kernels, one_kernel(): pl.pallas_call(functools.partial(mixer_kernel, blocks, groups), out_shape...  24.1 us
    unnamed x1, local copies, waits for them, and re-layouts  0.71 us

profile of v7, /device:TPU:0, one launch (start us, length us, event | category | flops | bytes accessed | tf_op | source)
XLA Modules:
  0.0 24.8 jit_solution(333574864560988363)
XLA Ops:
  0.0 24.1 %shard_map.109 = bf16[128,1024]{1,0:T(8,128)(2,1)S(1)} custom-call(bf16[128,1024]{1,0:T(8,128)(2,1)} %tokens_hbm.1, bf16[128,512]{1,0:T(8,128)(2,1)} %causal_hbm.1, bf16[128,512]{1,0:T(8,128)(2,1)} %anti_hbm.1, f32[3,1536]{1,0:T(4,128)} %conv_taps_hbm.1, f32[1,512]{1,0:T(1,128)} %bitcast.1, bf16[64,64]{1,0:T(8,128)(2,1)} %constant.8.clone.across_hbm, ...), custom_call_target="tpu_custom_call" | custom-call | tf_op jit(solution)/shard_map/pallas_call | solution.py:457
  24.1 0.7 %copy.13 = bf16[128,1024]{1,0:T(8,128)(2,1)} copy(bf16[128,1024]{1,0:T(8,128)(2,1)S(1)} %shard_map.109) | data formatting | bytes 524288

commit v8 on v7

--- a/solution.py
+++ b/solution.py
@@ -155,23 +155,26 @@
     return jnp.dot(gated, w_out, preferred_element_type=jnp.float32).astype(jnp.bfloat16)
 
 
-def grid_constants(blocks, width):
+def grid_constants(blocks, width, some):
     length = 2 * blocks * width
     half_freq = np.arange(blocks) + 0.5
-
+    each = np.eye(some)
     rows = np.outer(half_freq, np.arange(2 * blocks)) * (2.0 * np.pi / (2 * blocks))
     flip = np.where(np.arange(2 * blocks) < blocks, 1.0, -1.0)
     across = np.concatenate([np.cos(rows), -np.sin(rows)], axis=0) * flip
-    across = across.astype(ml_dtypes.bfloat16)
+    paired = across.reshape(2 * blocks, 2, blocks).transpose(0, 2, 1).reshape(across.shape)
     turn = np.outer(half_freq, np.arange(width)) * (2.0 * np.pi / length)
     twist = np.stack([np.cos(turn), np.sin(turn)]).astype(np.float32)
     grid = np.outer(np.arange(width), np.arange(width)) % width * (2.0 * np.pi / width)
     cos, sin = np.cos(grid), np.sin(grid)
-    within = np.block([[cos, -sin], [sin, cos]]).astype(np.float32)
+    within = np.block([[cos, -sin], [sin, cos]])
     back = rows[:, :blocks].T
     back = np.concatenate([np.cos(back), np.sin(back)], axis=1) * (2.0 / length)
-    back = back.astype(ml_dtypes.bfloat16)
-    return across, twist, within, back
+    mats = [np.kron(paired, each), np.kron(across[:, :blocks], each), within, np.kron(back, each)]
+    tiles = [np.split(mat, mat.shape[1] // 128, axis=1) for mat in mats]
+    packed = np.concatenate([tile for mat in tiles for tile in mat], axis=0)
+    shapes = [mat.shape for mat in mats]
+    return packed.astype(ml_dtypes.bfloat16), shapes, np.repeat(twist, some, axis=1)
 
 
 def dot32(a, b):
@@ -186,24 +189,22 @@
     anti_hbm,
     conv_taps_hbm,
     skip_gain_hbm,
-    across_hbm,
     twist_hbm,
-    back_hbm,
+    mats_hbm,
     w_in_hbm,
     w_out_hbm,
-    within_hbm,
     out,
     causal,
     anti,
     conv_taps,
     skip_gain,
-    across,
     twist,
+    over_filt,
+    over_sig,
+    within,
     back,
     w_in,
     w_out,
-    within_whole,
-    within,
     framed,
     edge_out,
     edge_in,
@@ -213,13 +214,7 @@
     sig_in,
     ret_out,
     ret_in,
-    spread,
-    gather,
-    result,
     spectrum,
-    gate,
-    passed,
-    gated,
     load_sem,
     edge_send,
     edge_recv,
@@ -244,55 +239,48 @@
         for step in range(groups):
             if turn > 0 or step > 0:
                 other = (fft + step) & (groups - 1)
-                peers.append((turn, level * groups + other, (level, other)))
+                peers.append((level * groups + other, (level, other)))
 
     barrier = pltpu.get_barrier_semaphore()
-    for _, _, coords in peers:
+    for _, coords in peers:
         pl.semaphore_signal(barrier, inc=1, device_id=coords, device_id_type=MESH)
 
+    pairs = [
+        (causal_hbm, causal),
+        (anti_hbm, anti),
+        (tokens_hbm, tokens),
+        (w_in_hbm, w_in),
+        (conv_taps_hbm, conv_taps),
+        (skip_gain_hbm, skip_gain),
+        (twist_hbm, twist),
+        (w_out_hbm, w_out),
+    ]
+    taken = 0
+    for mat in (over_filt, over_sig, within, back):
+        tall, wide = mat.shape
+        for start in range(0, wide, 128):
+            pairs.append((mats_hbm.at[pl.ds(taken, tall)], mat.at[:, pl.ds(start, 128)]))
+            taken += tall
     loads = [
-        pltpu.make_async_copy(src, dst, load_sem.at[i])
-        for i, (src, dst) in enumerate(
-            (
-                (causal_hbm, causal),
-                (anti_hbm, anti),
-                (tokens_hbm, tokens),
-                (w_in_hbm, w_in),
-                (conv_taps_hbm, conv_taps),
-                (across_hbm, across),
-                (twist_hbm, twist),
-                (within_hbm, within_whole),
-                (back_hbm, back),
-                (w_out_hbm, w_out),
-                (skip_gain_hbm, skip_gain),
-            )
-        )
+        pltpu.make_async_copy(src, dst, load_sem.at[i]) for i, (src, dst) in enumerate(pairs)
     ]
     for load in loads:
         load.start()
 
     def send_all(src, dst, send_sem, recv_sem):
-        for turn, peer, coords in peers:
+        for peer, coords in peers:
             pltpu.make_async_remote_copy(
                 src_ref=src.at[peer],
                 dst_ref=dst.at[me],
                 send_sem=send_sem,
-                recv_sem=recv_sem.at[turn],
+                recv_sem=recv_sem,
                 device_id=coords,
                 device_id_type=MESH,
             ).start()
-        pltpu.make_async_copy(src.at[me], dst.at[me], recv_sem.at[0]).start()
-
-    def plane_of(dst, turn):
-        return dst.at[pl.ds((blk ^ turn) * groups, groups)]
-
-    def arrived(dst, recv_sem, turn):
-        plane = plane_of(dst, turn)
-        pltpu.make_async_copy(plane, plane, recv_sem.at[turn]).wait()
+        pltpu.make_async_copy(src.at[me], dst.at[me], recv_sem).start()
 
     def all_arrived(dst, recv_sem):
-        for turn in range(levels):
-            arrived(dst, recv_sem, turn)
+        pltpu.make_async_copy(dst, dst, recv_sem).wait()
 
     def sent(src, send_sem):
         most = src.at[pl.ds(0, blocks - 1)]
@@ -369,49 +357,24 @@
     for load in loads[5:]:
         load.wait()
     second = stream(1)
-    direct = second * (skip_gain[...] * signal)
-    span = channels // levels
-    for level in range(levels):
-        gate[level] = second[:, level * span : (level + 1) * span]
-        passed[level] = direct[:, level * span : (level + 1) * span]
-    within[...] = within_whole[...].astype(bf16)
+    direct = skip_gain[...] * signal
     cos, sin = twist[0], twist[1]
+    half = blocks * some
 
     def twisted(real, imag, axis):
-        return jnp.concatenate([real * cos + imag * sin, imag * cos - real * sin], axis=axis)
-
-    def lane(x, c):
-        return x[:, c * width : (c + 1) * width]
-
-    def forward(columns, mats):
-        freq = dot32(mats, jnp.concatenate(columns, axis=1))
-        turned = [
-            twisted(lane(freq[:blocks], c), lane(freq[blocks:], c), 1)
-            for c in range(len(columns))
-        ]
-        return dot32(jnp.concatenate(turned, axis=0).astype(bf16), within[...])
+        return jnp.concatenate(
+            [real * cos + imag * sin, imag * cos - real * sin], axis=axis
+        ).astype(bf16)
+
+    def forward(rows, mat):
+        freq = dot32(mat[...], rows)
+        return dot32(twisted(freq[:half], freq[half:], 1), within[...])
 
     for part in range(parts):
         all_arrived(filt_in.at[part], filt_recv.at[part])
-        spread[...] = filt_in[part].astype(f32).reshape(2 * blocks * some, width)
-        columns = [
-            jnp.concatenate(
-                [
-                    spread[pl.ds(c, blocks, stride=2 * some), :],
-                    spread[pl.ds(some + c, blocks, stride=2 * some), :],
-                ],
-                axis=0,
-            ).astype(bf16)
-            for c in range(some)
-        ]
-        spectrum[...] = forward(columns, across[...])
-
+        spectrum[...] = forward(filt_in[part].reshape(2 * half, width), over_filt)
         all_arrived(sig_in.at[part], sig_recv.at[part])
-        gather[...] = sig_in[part].astype(f32).reshape(blocks * some, width)
-        columns = [
-            gather[pl.ds(c, blocks, stride=some), :].astype(bf16) for c in range(some)
-        ]
-        freq = forward(columns, across[:, 0:blocks])
+        freq = forward(sig_in[part].reshape(half, width), over_sig)
         s_real, s_imag = freq[:, :width], freq[:, width:]
         f_real, f_imag = spectrum[:, :width], spectrum[:, width:]
         product = jnp.concatenate(
@@ -419,23 +382,15 @@
             axis=1,
         )
         turned = dot32(product.astype(bf16), within[...])
-        pieces = [turned[i * blocks : (i + 1) * blocks] for i in range(some)]
-        pieces = [twisted(x[:, :width], x[:, width:], 0) for x in pieces]
-        conv = dot32(back[...], jnp.concatenate(pieces, axis=1).astype(bf16))
-        for c in range(some):
-            result[pl.ds(c, blocks, stride=some), :] = lane(conv, c)
-        ret_out[part] = result[...].astype(bf16).reshape(blocks, some, width)
+        conv = dot32(back[...], twisted(turned[:, :width], turned[:, width:], 0))
+        ret_out[part] = conv.astype(bf16).reshape(blocks, some, width)
         send_part(ret, part)
 
-    for turn in range(levels):
-        level = blk ^ turn
-        for part in range(parts):
-            arrived(ret_in.at[part], ret_recv.at[part], turn)
-        landed = [plane_of(ret_in.at[part], turn)[...].astype(f32) for part in range(parts)]
-        landed = jnp.concatenate(landed, axis=1).reshape(span, width).T
-        cols = pl.ds(pl.multiple_of(level * span, span), span)
-        gated[:, cols] = (gate[level] * landed + passed[level]).astype(bf16)
-    out[...] = dot32(gated[...], w_out[...]).astype(bf16)
+    for part in range(parts):
+        all_arrived(ret_in.at[part], ret_recv.at[part])
+    landed = jnp.concatenate([ret_in[part].astype(f32) for part in range(parts)], axis=1)
+    convolved = landed.reshape(channels, width).T + direct
+    out[...] = dot32((second * convolved).astype(bf16), w_out[...]).astype(bf16)
     for src, _, send_sem, _ in (filt, sig, ret):
         for part in range(parts):
             sent(src.at[part], send_sem.at[part])
@@ -446,10 +401,9 @@
     channels = w_out.shape[0]
     groups = lax.axis_size("fft")
     blocks = lax.axis_size("blk") * groups
-    levels = lax.axis_size("blk")
     parts = 2
     some = channels // blocks // parts
-    across, twist, within, back = grid_constants(blocks, width)
+    packed, shapes, twist = grid_constants(blocks, width, some)
     f32, bf16 = jnp.float32, jnp.bfloat16
     vmem = pl.BlockSpec(memory_space=pltpu.VMEM)
     hbm = pl.BlockSpec(memory_space=pl.ANY)
@@ -457,20 +411,20 @@
     return pl.pallas_call(
         functools.partial(mixer_kernel, blocks, groups),
         out_shape=pltpu.VMEM((width, w_out.shape[1]), bf16),
-        in_specs=[hbm] * 11,
+        in_specs=[hbm] * 9,
         out_specs=vmem,
         scratch_shapes=[
             pltpu.VMEM(causal_taps.shape, bf16),
             pltpu.VMEM(anticausal_taps.shape, bf16),
             pltpu.VMEM(conv_taps.shape, f32),
             pltpu.VMEM((1, channels), f32),
-            pltpu.VMEM(across.shape, bf16),
             pltpu.VMEM(twist.shape, f32),
-            pltpu.VMEM(back.shape, bf16),
+            pltpu.VMEM(shapes[0], bf16),
+            pltpu.VMEM(shapes[1], bf16),
+            pltpu.VMEM(shapes[2], bf16),
+            pltpu.VMEM(shapes[3], bf16),
             pltpu.VMEM(w_in.shape, bf16),
             pltpu.VMEM(w_out.shape, bf16),
-            pltpu.VMEM(within.shape, f32),
-            pltpu.VMEM(within.shape, bf16),
             pltpu.VMEM((width + 16, depth), bf16),
             pltpu.VMEM((2, 1, depth), f32),
             pltpu.VMEM((2, 1, depth), f32),
@@ -480,22 +434,16 @@
             pltpu.VMEM((parts, blocks, some, width), bf16),
             pltpu.VMEM((parts, blocks, some, width), bf16),
             pltpu.VMEM((parts, blocks, some, width), bf16),
-            pltpu.VMEM((2 * blocks * some, width), f32),
-            pltpu.VMEM((blocks * some, width), f32),
-            pltpu.VMEM((blocks * some, width), f32),
             pltpu.VMEM((some * blocks, 2 * width), f32),
-            pltpu.VMEM((levels, width, channels // levels), f32),
-            pltpu.VMEM((levels, width, channels // levels), f32),
-            pltpu.VMEM((width, channels), bf16),
-            one((11,)),
+            one((8 + sum(wide // 128 for _, wide in shapes),)),
             one((2,)),
             one((2,)),
             one((parts,)),
-            one((parts, levels)),
-            one((parts,)),
-            one((parts, levels)),
-            one((parts,)),
-            one((parts, levels)),
+            one((parts,)),
+            one((parts,)),
+            one((parts,)),
+            one((parts,)),
+            one((parts,)),
         ],
         compiler_params=pltpu.CompilerParams(
             collective_id=0, has_side_effects=True, vmem_limit_bytes=62 * 2**20
@@ -506,12 +454,10 @@
         anticausal_taps,
         conv_taps,
         skip_gain[None, :],
-        jnp.asarray(across),
         jnp.asarray(twist),
-        jnp.asarray(back),
+        jnp.asarray(packed),
         w_in,
         w_out,
-        jnp.asarray(within),
     )
 
 

time: 24.9 us -> 25.1 us (level)
  no operation moved by 1% of the time
where the time goes in v8:
time: 25.1 us; the launch traced here: 25 us
  Pallas kernels  24.3 us (97%)
  local copies, waits for them, and re-layouts  0.71 us (3%)
    pallas_call x1, Pallas kernels, one_kernel(): pl.pallas_call(functools.partial(mixer_kernel, blocks, groups), out_shape...  24.3 us
    unnamed x1, local copies, waits for them, and re-layouts  0.71 us

profile of v8, /device:TPU:0, one launch (start us, length us, event | category | flops | bytes accessed | tf_op | source)
XLA Modules:
  0.0 25.0 jit_solution(15630754550024584279)
XLA Ops:
  0.0 24.3 %shard_map.91 = bf16[128,1024]{1,0:T(8,128)(2,1)S(1)} custom-call(bf16[128,1024]{1,0:T(8,128)(2,1)} %tokens_hbm.1, bf16[128,512]{1,0:T(8,128)(2,1)} %causal_hbm.1, bf16[128,512]{1,0:T(8,128)(2,1)} %anti_hbm.1, f32[3,1536]{1,0:T(4,128)} %conv_taps_hbm.1, f32[1,512]{1,0:T(1,128)} %bitcast.1, f32[2,256,128]{2,1,0:T(8,128)} %constant.4.clone.twist_hbm, ...), custom_call_target="tpu_custom_call" | custom-call | tf_op jit(solution)/shard_map/pallas_call | solution.py:411
  24.3 0.7 %copy.11 = bf16[128,1024]{1,0:T(8,128)(2,1)} copy(bf16[128,1024]{1,0:T(8,128)(2,1)S(1)} %shard_map.91) | data formatting | bytes 524288

commit v9 on v8

--- a/solution.py
+++ b/solution.py
@@ -401,7 +401,7 @@
     channels = w_out.shape[0]
     groups = lax.axis_size("fft")
     blocks = lax.axis_size("blk") * groups
-    parts = 2
+    parts = 1
     some = channels // blocks // parts
     packed, shapes, twist = grid_constants(blocks, width, some)
     f32, bf16 = jnp.float32, jnp.bfloat16

time: 25.1 us -> 26.3 us (1.048)
  Pallas kernels: 24.3 us -> 25.5 us
    pallas_call x1, Pallas kernels: 24.3 us -> 25.5 us  [one_kernel(): pl.pallas_call(functools.partial(mixer_kernel, blocks, groups), out_shape...]
where the time goes in v9:
time: 26.3 us; the launch traced here: 26.2 us
  Pallas kernels  25.5 us (97%)
  local copies, waits for them, and re-layouts  0.71 us (3%)
    pallas_call x1, Pallas kernels, one_kernel(): pl.pallas_call(functools.partial(mixer_kernel, blocks, groups), out_shape...  25.5 us
    unnamed x1, local copies, waits for them, and re-layouts  0.71 us

profile of v9, /device:TPU:0, one launch (start us, length us, event | category | flops | bytes accessed | tf_op | source)
XLA Modules:
  0.0 26.2 jit_solution(3835659834500592394)
XLA Ops:
  0.0 25.5 %shard_map.91 = bf16[128,1024]{1,0:T(8,128)(2,1)S(1)} custom-call(bf16[128,1024]{1,0:T(8,128)(2,1)} %tokens_hbm.1, bf16[128,512]{1,0:T(8,128)(2,1)} %causal_hbm.1, bf16[128,512]{1,0:T(8,128)(2,1)} %anti_hbm.1, f32[3,1536]{1,0:T(4,128)} %conv_taps_hbm.1, f32[1,512]{1,0:T(1,128)} %bitcast.1, f32[2,512,128]{2,1,0:T(8,128)} %constant.4.clone.twist_hbm, ...), custom_call_target="tpu_custom_call" | custom-call | tf_op jit(solution)/shard_map/pallas_call | solution.py:411
  25.5 0.7 %copy.11 = bf16[128,1024]{1,0:T(8,128)(2,1)} copy(bf16[128,1024]{1,0:T(8,128)(2,1)S(1)} %shard_map.91) | data formatting | bytes 524288

commit v10 on v7

--- a/solution.py
+++ b/solution.py
@@ -217,9 +217,6 @@
     gather,
     result,
     spectrum,
-    gate,
-    passed,
-    gated,
     load_sem,
     edge_send,
     edge_recv,
@@ -244,10 +241,10 @@
         for step in range(groups):
             if turn > 0 or step > 0:
                 other = (fft + step) & (groups - 1)
-                peers.append((turn, level * groups + other, (level, other)))
+                peers.append((level * groups + other, (level, other)))
 
     barrier = pltpu.get_barrier_semaphore()
-    for _, _, coords in peers:
+    for _, coords in peers:
         pl.semaphore_signal(barrier, inc=1, device_id=coords, device_id_type=MESH)
 
     loads = [
@@ -272,27 +269,19 @@
         load.start()
 
     def send_all(src, dst, send_sem, recv_sem):
-        for turn, peer, coords in peers:
+        for peer, coords in peers:
             pltpu.make_async_remote_copy(
                 src_ref=src.at[peer],
                 dst_ref=dst.at[me],
                 send_sem=send_sem,
-                recv_sem=recv_sem.at[turn],
+                recv_sem=recv_sem,
                 device_id=coords,
                 device_id_type=MESH,
             ).start()
-        pltpu.make_async_copy(src.at[me], dst.at[me], recv_sem.at[0]).start()
-
-    def plane_of(dst, turn):
-        return dst.at[pl.ds((blk ^ turn) * groups, groups)]
-
-    def arrived(dst, recv_sem, turn):
-        plane = plane_of(dst, turn)
-        pltpu.make_async_copy(plane, plane, recv_sem.at[turn]).wait()
+        pltpu.make_async_copy(src.at[me], dst.at[me], recv_sem).start()
 
     def all_arrived(dst, recv_sem):
-        for turn in range(levels):
-            arrived(dst, recv_sem, turn)
+        pltpu.make_async_copy(dst, dst, recv_sem).wait()
 
     def sent(src, send_sem):
         most = src.at[pl.ds(0, blocks - 1)]
@@ -369,11 +358,7 @@
     for load in loads[5:]:
         load.wait()
     second = stream(1)
-    direct = second * (skip_gain[...] * signal)
-    span = channels // levels
-    for level in range(levels):
-        gate[level] = second[:, level * span : (level + 1) * span]
-        passed[level] = direct[:, level * span : (level + 1) * span]
+    direct = skip_gain[...] * signal
     within[...] = within_whole[...].astype(bf16)
     cos, sin = twist[0], twist[1]
 
@@ -427,15 +412,11 @@
         ret_out[part] = result[...].astype(bf16).reshape(blocks, some, width)
         send_part(ret, part)
 
-    for turn in range(levels):
-        level = blk ^ turn
-        for part in range(parts):
-            arrived(ret_in.at[part], ret_recv.at[part], turn)
-        landed = [plane_of(ret_in.at[part], turn)[...].astype(f32) for part in range(parts)]
-        landed = jnp.concatenate(landed, axis=1).reshape(span, width).T
-        cols = pl.ds(pl.multiple_of(level * span, span), span)
-        gated[:, cols] = (gate[level] * landed + passed[level]).astype(bf16)
-    out[...] = dot32(gated[...], w_out[...]).astype(bf16)
+    for part in range(parts):
+        all_arrived(ret_in.at[part], ret_recv.at[part])
+    landed = jnp.concatenate([ret_in[part].astype(f32) for part in range(parts)], axis=1)
+    convolved = landed.reshape(channels, width).T + direct
+    out[...] = dot32((second * convolved).astype(bf16), w_out[...]).astype(bf16)
     for src, _, send_sem, _ in (filt, sig, ret):
         for part in range(parts):
             sent(src.at[part], send_sem.at[part])
@@ -446,7 +427,6 @@
     channels = w_out.shape[0]
     groups = lax.axis_size("fft")
     blocks = lax.axis_size("blk") * groups
-    levels = lax.axis_size("blk")
     parts = 2
     some = channels // blocks // parts
     across, twist, within, back = grid_constants(blocks, width)
@@ -484,18 +464,15 @@
             pltpu.VMEM((blocks * some, width), f32),
             pltpu.VMEM((blocks * some, width), f32),
             pltpu.VMEM((some * blocks, 2 * width), f32),
-            pltpu.VMEM((levels, width, channels // levels), f32),
-            pltpu.VMEM((levels, width, channels // levels), f32),
-            pltpu.VMEM((width, channels), bf16),
             one((11,)),
             one((2,)),
             one((2,)),
             one((parts,)),
-            one((parts, levels)),
             one((parts,)),
-            one((parts, levels)),
             one((parts,)),
-            one((parts, levels)),
+            one((parts,)),
+            one((parts,)),
+            one((parts,)),
         ],
         compiler_params=pltpu.CompilerParams(
             collective_id=0, has_side_effects=True, vmem_limit_bytes=62 * 2**20

time: 24.9 us -> 24.8 us (level)
  no operation moved by 1% of the time
where the time goes in v10:
time: 24.8 us; the launch traced here: 24.6 us
  Pallas kernels  23.9 us (96%)
  local copies, waits for them, and re-layouts  0.71 us (3%)
    pallas_call x1, Pallas kernels, one_kernel(): pl.pallas_call(functools.partial(mixer_kernel, blocks, groups), out_shape...  23.9 us
    unnamed x1, local copies, waits for them, and re-layouts  0.71 us

profile of v10, /device:TPU:0, one launch (start us, length us, event | category | flops | bytes accessed | tf_op | source)
XLA Modules:
  0.0 24.6 jit_solution(15180000179190166881)
XLA Ops:
  0.0 23.9 %shard_map.109 = bf16[128,1024]{1,0:T(8,128)(2,1)S(1)} custom-call(bf16[128,1024]{1,0:T(8,128)(2,1)} %tokens_hbm.1, bf16[128,512]{1,0:T(8,128)(2,1)} %causal_hbm.1, bf16[128,512]{1,0:T(8,128)(2,1)} %anti_hbm.1, f32[3,1536]{1,0:T(4,128)} %conv_taps_hbm.1, f32[1,512]{1,0:T(1,128)} %bitcast.1, bf16[64,64]{1,0:T(8,128)(2,1)} %constant.8.clone.across_hbm, ...), custom_call_target="tpu_custom_call" | custom-call | tf_op jit(solution)/shard_map/pallas_call | solution.py:437
  23.9 0.7 %copy.13 = bf16[128,1024]{1,0:T(8,128)(2,1)} copy(bf16[128,1024]{1,0:T(8,128)(2,1)S(1)} %shard_map.109) | data formatting | bytes 524288

commit v11 on v10

--- a/solution.py
+++ b/solution.py
@@ -322,7 +322,8 @@
     filt = (filt_out, filt_in, filt_send, filt_recv)
     sig = (sig_out, sig_in, sig_send, sig_recv)
     ret = (ret_out, ret_in, ret_send, ret_recv)
-    send_part(filt, 0)
+    for part in range(parts):
+        send_part(filt, part)
 
     for load in loads[3:5]:
         load.wait()
@@ -352,8 +353,6 @@
     for part in range(parts):
         sig_out[part] = signal_rows[:, part].astype(bf16)
         send_part(sig, part)
-        if part + 1 < parts:
-            send_part(filt, part + 1)
 
     for load in loads[5:]:
         load.wait()

time: 24.8 us -> 25.4 us (1.024)
  Pallas kernels: 23.9 us -> 24.5 us
    pallas_call x1, Pallas kernels: 23.9 us -> 24.5 us  [one_kernel(): pl.pallas_call(functools.partial(mixer_kernel, blocks, groups), out_shape...]
where the time goes in v11:
time: 25.4 us; the launch traced here: 25.3 us
  Pallas kernels  24.5 us (96%)
  local copies, waits for them, and re-layouts  0.71 us (3%)
    pallas_call x1, Pallas kernels, one_kernel(): pl.pallas_call(functools.partial(mixer_kernel, blocks, groups), out_shape...  24.5 us
    unnamed x1, local copies, waits for them, and re-layouts  0.71 us

profile of v11, /device:TPU:0, one launch (start us, length us, event | category | flops | bytes accessed | tf_op | source)
XLA Modules:
  0.0 25.3 jit_solution(15738663549182908442)
XLA Ops:
  0.0 24.5 %shard_map.109 = bf16[128,1024]{1,0:T(8,128)(2,1)S(1)} custom-call(bf16[128,1024]{1,0:T(8,128)(2,1)} %tokens_hbm.1, bf16[128,512]{1,0:T(8,128)(2,1)} %causal_hbm.1, bf16[128,512]{1,0:T(8,128)(2,1)} %anti_hbm.1, f32[3,1536]{1,0:T(4,128)} %conv_taps_hbm.1, f32[1,512]{1,0:T(1,128)} %bitcast.1, bf16[64,64]{1,0:T(8,128)(2,1)} %constant.8.clone.across_hbm, ...), custom_call_target="tpu_custom_call" | custom-call | tf_op jit(solution)/shard_map/pallas_call | solution.py:436
  24.6 0.7 %copy.13 = bf16[128,1024]{1,0:T(8,128)(2,1)} copy(bf16[128,1024]{1,0:T(8,128)(2,1)S(1)} %shard_map.109) | data formatting | bytes 524288
